TPU v7x, 32 devices: a whole 2x2x4 slice. The times are simulated.
32 devices in a mesh: dp: 4 (over z), seq: 4 (over x, core), expert: 2 (over y).
Axes of the slice: x: 2, y: 2, z: 4, core: 2. Of those that a mesh axis runs over, the one named last changes fastest.
Arguments:
- tokens: bfloat16 [16, 1024, 768], P(('dp', 'expert'), 'seq'), may hold values from -6 to 6
- token_ids: int32 [16, 1024], P(('dp', 'expert'), 'seq'), may hold values from 0 to 8191, as said below
- hash_table: int32 [8192], replicated, may hold values from 0 to 1, as said below
- lengths: int32 [16, 2], P(('dp', 'expert')), may hold values from 0 to 1024, as said below
- gain_attn: float32 [768], replicated, may hold values from 0.5 to 1.5
- w_query: bfloat16 [768, 768], replicated, may hold values from -0.21875 to 0.21875
- w_key: bfloat16 [768, 768], replicated, may hold values from -0.21875 to 0.21875
- w_value: bfloat16 [768, 768], replicated, may hold values from -0.21875 to 0.21875
- w_output: bfloat16 [768, 768], replicated, may hold values from -1.25 to 1.25
- gain_ffn: float32 [768], replicated, may hold values from 0.5 to 1.5
- w_in: bfloat16 [2, 768, 3072], P('expert', None, 'seq'), may hold values from -0.21875 to 0.21875
- w_out: bfloat16 [2, 3072, 768], P('expert', 'seq'), may hold values from -0.109375 to 0.109375
- cotangent: bfloat16 [16, 1024, 768], P(('dp', 'expert'), 'seq'), may hold values from -6 to 6
Outputs:
- output: bfloat16 [16, 1024, 768], P(('dp', 'expert'), 'seq')
- input_grad: float32 [16, 1024, 768], P(('dp', 'expert'), 'seq')
- grad_gain_attn: float32 [768], replicated
- grad_query: float32 [768, 768], replicated
- grad_key: float32 [768, 768], replicated
- grad_value: float32 [768, 768], replicated
- grad_output: float32 [768, 768], replicated
- grad_gain_ffn: float32 [768], replicated
- grad_in: float32 [2, 768, 3072], P('expert', None, 'seq')
- grad_out: float32 [2, 3072, 768], P('expert', 'seq')
Inputs may be any that keep to these rules, and one draw needn't show every extreme that they name: `token_ids`: among the 512 tokens of one device (positions s * 256 to (s + 1) * 256 - 1 of each of its 2 rows), at most 384 are hashed to any one expert; on every device exactly 384 are hashed to one expert, and that expert is the same on all devices that share a dp index and a seq index. `hash_table`: each expert is the image of 4096 token ids. `lengths`: each row holds either one document of 1024 positions (its second length is 0) or two documents of 512 positions; among the 2 rows that one device holds, at least one is a single document.
All inputs are finite; a program needn't handle non-finite values.
Results may differ from a plain program's by a relative error of at most 0.015.
Values may be sent and summed in bfloat16 or wider, within the bound.
A program may use at most 192 MiB of HBM per device.

v0:
```python
import jax
import jax.numpy as jnp
from jax import lax
from jax.sharding import PartitionSpec as P

H = 12
HD = 64


epsilon = 1e-05
masked_score = -1e30


def norm_rows(values, gain):
    average = jnp.mean(values, axis=-1, keepdims=True)
    centred = values - average
    spread = jnp.mean(centred * centred, axis=-1, keepdims=True)
    return centred * lax.rsqrt(spread + epsilon) * gain


def gelu_grad(pre, upstream):
    unused, pullback = jax.vjp(jax.nn.gelu, pre)
    return pullback(upstream)[0]


def split_heads(matrix):
    return matrix.reshape(matrix.shape[0], matrix.shape[1], H, HD).transpose(2, 0, 1, 3)


def join_heads(stacked):
    return stacked.transpose(1, 2, 0, 3).reshape(stacked.shape[1], stacked.shape[2], H * HD)


def per_device(
    tokens,
    token_ids,
    hash_table,
    lengths,
    gain_attn,
    w_query,
    w_key,
    w_value,
    w_output,
    gain_ffn,
    w_in,
    w_out,
    cotangent,
):
    row_count, span, width = tokens.shape
    local_tok = row_count * span
    whole = span * lax.axis_size("seq")
    place = lax.axis_index("seq")
    scale = HD ** (-0.5)
    inputs = tokens.reshape(local_tok, width).astype(jnp.float32)
    key_positions = jnp.arange(whole, dtype=jnp.int32)
    query_positions = place * span + jnp.arange(span, dtype=jnp.int32)
    ends = jnp.cumsum(lengths, axis=1)
    key_document = jnp.sum(
        (key_positions[None, :, None] >= ends[:, None, :]).astype(jnp.int32), axis=2
    )
    query_document = jnp.sum(
        (query_positions[None, :, None] >= ends[:, None, :]).astype(jnp.int32), axis=2
    )
    visible = (key_positions[None, None, :] <= query_positions[None, :, None]) & (
        query_document[:, :, None] == key_document[:, None, :]
    )
    normed, first_norm_back = jax.vjp(norm_rows, inputs, gain_attn)
    normed_low = normed.astype(jnp.bfloat16)
    query = jnp.dot(normed_low, w_query, preferred_element_type=jnp.float32).astype(jnp.bfloat16)
    keys = jnp.dot(normed_low, w_key, preferred_element_type=jnp.float32).astype(jnp.bfloat16)
    values = jnp.dot(normed_low, w_value, preferred_element_type=jnp.float32).astype(jnp.bfloat16)
    own_pair = jnp.concatenate([keys, values], axis=1).reshape(row_count, span, 2 * width)
    all_pairs = lax.all_gather(own_pair, "seq", axis=1, tiled=True)

    def pair_heads(pairs):
        return (split_heads(pairs[:, :, :width]), split_heads(pairs[:, :, width:]))

    query_heads = split_heads(query.reshape(row_count, span, width))
    key_heads, value_heads = pair_heads(all_pairs)

    def head_forward(parts):
        query_one, key_one, value_one = parts
        scores = (
            jnp.einsum("rqd,rkd->rqk", query_one, key_one, preferred_element_type=jnp.float32)
            * scale
        )
        scores = jnp.where(visible, scores, masked_score)
        peak = jnp.max(scores, axis=2, keepdims=True)
        weights = jnp.exp(scores - peak)
        totals = jnp.sum(weights, axis=2, keepdims=True)
        probs = (weights / totals).astype(jnp.bfloat16)
        mixed = jnp.einsum("rqk,rkd->rqd", probs, value_one, preferred_element_type=jnp.float32)
        return (mixed, (peak + jnp.log(totals))[:, :, 0])

    mixed_heads, log_totals = lax.map(head_forward, (query_heads, key_heads, value_heads))
    attended = join_heads(mixed_heads).reshape(local_tok, width).astype(jnp.bfloat16)
    middle = inputs + jnp.dot(attended, w_output, preferred_element_type=jnp.float32)
    ffn_norm, second_norm_back = jax.vjp(norm_rows, middle, gain_ffn)
    ffn_in = ffn_norm.astype(jnp.bfloat16)
    experts = lax.axis_size("expert")
    capacity = min(2 * local_tok // experts, 3 * local_tok // 4)
    expert_of = jnp.take(hash_table, token_ids.reshape(local_tok), axis=0)
    labels = jnp.arange(experts, dtype=jnp.int32)
    onehot = (expert_of[:, None] == labels[None, :]).astype(jnp.int32)
    own_rank = jnp.sum((jnp.cumsum(onehot, axis=0) - 1) * onehot, axis=1)
    slots = expert_of * capacity + own_rank
    sources = (
        jnp.full((experts * capacity,), local_tok, jnp.int32)
        .at[slots]
        .set(jnp.arange(local_tok, dtype=jnp.int32))
    )

    def to_slots(rows_low):
        padded = jnp.concatenate([rows_low, jnp.zeros((1, width), rows_low.dtype)], axis=0)
        return jnp.take(padded, sources, axis=0).reshape(experts, capacity, width)

    received = lax.all_to_all(
        to_slots(ffn_in), "expert", split_axis=0, concat_axis=0, tiled=True
    ).reshape(-1, width)
    full_in, full_out = (
        lax.all_gather(w_in, "seq", axis=2, tiled=True),
        lax.all_gather(w_out, "seq", axis=1, tiled=True),
    )
    full_in = full_in[0]
    full_out = full_out[0]
    first = jnp.dot(received, full_in, preferred_element_type=jnp.float32)
    produced = jnp.dot(
        jax.nn.gelu(first).astype(jnp.bfloat16), full_out, preferred_element_type=jnp.float32
    ).astype(jnp.bfloat16)
    returned = lax.all_to_all(
        produced.reshape(experts, capacity, width),
        "expert",
        split_axis=0,
        concat_axis=0,
        tiled=True,
    ).reshape(-1, width)
    output = middle + jnp.take(returned, slots, axis=0).astype(jnp.float32)
    upstream = cotangent.reshape(local_tok, width)
    grad_received_out = lax.all_to_all(
        to_slots(upstream), "expert", split_axis=0, concat_axis=0, tiled=True
    ).reshape(-1, width)
    pre = jnp.dot(received, full_in, preferred_element_type=jnp.float32)
    hidden = jax.nn.gelu(pre).astype(jnp.bfloat16)
    grad_full_out = jnp.einsum(
        "rf,rd->fd", hidden, grad_received_out, preferred_element_type=jnp.float32
    )
    grad_hidden = jnp.einsum(
        "rd,fd->rf", grad_received_out, full_out, preferred_element_type=jnp.float32
    )
    grad_pre = gelu_grad(pre, grad_hidden).astype(jnp.bfloat16)
    grad_full_in = jnp.einsum("rd,rf->df", received, grad_pre, preferred_element_type=jnp.float32)
    grad_received = jnp.einsum(
        "rf,df->rd", grad_pre, full_in, preferred_element_type=jnp.float32
    ).astype(jnp.bfloat16)
    grad_in_part, grad_out_part = (
        lax.psum_scatter(
            grad_full_in[None].astype(jnp.bfloat16), "seq", scatter_dimension=2, tiled=True
        ).astype(jnp.float32),
        lax.psum_scatter(
            grad_full_out[None].astype(jnp.bfloat16), "seq", scatter_dimension=1, tiled=True
        ).astype(jnp.float32),
    )
    grad_in, grad_out = (
        lax.psum(grad_in_part.astype(jnp.bfloat16), "dp").astype(jnp.float32),
        lax.psum(grad_out_part.astype(jnp.bfloat16), "dp").astype(jnp.float32),
    )
    grad_back = lax.all_to_all(
        grad_received.reshape(experts, capacity, width),
        "expert",
        split_axis=0,
        concat_axis=0,
        tiled=True,
    ).reshape(-1, width)
    grad_ffn_in = jnp.take(grad_back, slots, axis=0).astype(jnp.float32)
    grad_middle_norm, grad_gain_ffn = second_norm_back(grad_ffn_in)
    grad_middle = upstream.astype(jnp.float32) + grad_middle_norm
    grad_branch = grad_middle.astype(jnp.bfloat16)
    grad_w_output = jnp.einsum(
        "cd,ce->de", attended, grad_branch, preferred_element_type=jnp.float32
    )
    grad_attended = jnp.einsum(
        "ce,de->cd", grad_branch, w_output, preferred_element_type=jnp.float32
    ).astype(jnp.bfloat16)
    again_pairs = lax.all_gather(own_pair, "seq", axis=1, tiled=True)
    key_back, value_back = pair_heads(again_pairs)

    def head_backward(parts):
        query_one, key_one, value_one, grad_one, log_one = parts
        scores = (
            jnp.einsum("rqd,rkd->rqk", query_one, key_one, preferred_element_type=jnp.float32)
            * scale
        )
        scores = jnp.where(visible, scores, masked_score)
        probs_full = jnp.exp(scores - log_one[:, :, None])
        probs = probs_full.astype(jnp.bfloat16)
        grad_probs = jnp.einsum(
            "rqd,rkd->rqk", grad_one, value_one, preferred_element_type=jnp.float32
        )
        inner = jnp.sum(probs_full * grad_probs, axis=2, keepdims=True)
        grad_scores = (probs_full * (grad_probs - inner)).astype(jnp.bfloat16)
        grad_query_one = (
            jnp.einsum("rqk,rkd->rqd", grad_scores, key_one, preferred_element_type=jnp.float32)
            * scale
        )
        grad_key_one = (
            jnp.einsum("rqk,rqd->rkd", grad_scores, query_one, preferred_element_type=jnp.float32)
            * scale
        )
        grad_value_one = jnp.einsum(
            "rqk,rqd->rkd", probs, grad_one, preferred_element_type=jnp.float32
        )
        return (grad_query_one, grad_key_one, grad_value_one)

    grad_att_heads = split_heads(grad_attended.reshape(row_count, span, width))
    grad_query_heads, grad_key_heads, grad_value_heads = lax.map(
        head_backward, (query_heads, key_back, value_back, grad_att_heads, log_totals)
    )
    grad_query_rows = join_heads(grad_query_heads).reshape(local_tok, width).astype(jnp.bfloat16)
    pair_grads = jnp.concatenate([join_heads(grad_key_heads), join_heads(grad_value_heads)], axis=2)
    own_grads = (
        lax.psum_scatter(pair_grads, "seq", scatter_dimension=1, tiled=True)
        .reshape(local_tok, 2 * width)
        .astype(jnp.bfloat16)
    )
    grad_key_rows = own_grads[:, :width]
    grad_value_rows = own_grads[:, width:]
    grad_w_query = jnp.einsum(
        "cd,ce->de", normed_low, grad_query_rows, preferred_element_type=jnp.float32
    )
    grad_w_key = jnp.einsum(
        "cd,ce->de", normed_low, grad_key_rows, preferred_element_type=jnp.float32
    )
    grad_w_value = jnp.einsum(
        "cd,ce->de", normed_low, grad_value_rows, preferred_element_type=jnp.float32
    )
    grad_normed = jnp.einsum(
        "ce,de->cd", grad_query_rows, w_query, preferred_element_type=jnp.float32
    )
    grad_normed = grad_normed + jnp.einsum(
        "ce,de->cd", grad_key_rows, w_key, preferred_element_type=jnp.float32
    )
    grad_normed = grad_normed + jnp.einsum(
        "ce,de->cd", grad_value_rows, w_value, preferred_element_type=jnp.float32
    )
    grad_inputs_norm, grad_gain_attn = first_norm_back(grad_normed)
    input_grad = grad_middle + grad_inputs_norm
    summed = lax.psum(
        (grad_gain_attn, grad_w_query, grad_w_key, grad_w_value, grad_w_output, grad_gain_ffn),
        ("dp", "seq", "expert"),
    )
    shaped_output = output.astype(jnp.bfloat16).reshape(row_count, span, width)
    shaped_grad = input_grad.reshape(row_count, span, width)
    return (
        shaped_output,
        shaped_grad,
        summed[0],
        summed[1],
        summed[2],
        summed[3],
        summed[4],
        summed[5],
        grad_in,
        grad_out,
    )


def solution(mesh):
    return jax.shard_map(
        per_device,
        mesh=mesh,
        in_specs=(
            P(("dp", "expert"), "seq", None),
            P(("dp", "expert"), "seq"),
            P(),
            P(("dp", "expert"), None),
            P(),
            P(),
            P(),
            P(),
            P(),
            P(),
            P("expert", None, "seq"),
            P("expert", "seq", None),
            P(("dp", "expert"), "seq", None),
        ),
        out_specs=(
            P(("dp", "expert"), "seq", None),
            P(("dp", "expert"), "seq", None),
            P(),
            P(),
            P(),
            P(),
            P(),
            P(),
            P("expert", None, "seq"),
            P("expert", "seq", None),
        ),
        check_vma=False,
    )
```

profile of v0, /device:TPU:0, one launch (start us, length us, event | category | flops | bytes accessed | tf_op | source)
XLA Modules:
  0.0 798.7 jit_solution(14271883651491163324)
XLA Ops:
  42.7 26.1 %all-gather.4.cloned.1.call-done = bf16[2,1024,1536]{1,2,0:T(8,128)(2,1)} async-done(((bf16[2,256,1536]{1,2,0:T(8,128)(2,1)}), bf16[2,1024,1536]{1,2,0:T(8,128)(2,1)}) %all-gather.4.cloned.1.call-update) | async-done | bytes 6291472 | tf_op jit(solution)/shard_map/all_gather | solution.py:73
  68.9 3.6 fusion.99
  76.9 54.4 %while.28 = (s32[]{:T(128)}, bf16[12,2,256,64]{2,3,1,0:T(8,128)(2,1)S(1)}, f32[12,2,256]{2,1,0:T(2,128)}, bf16[12,2,256,64]{2,3,1,0:T(8,128)(2,1)}, bf16[12,2,10...) while((s32[]{:T(128)}, ...), condition=%wide.region_8.9_spmd.clone, body=%wide.region_5.8_spmd.clone.sunk | while | flops 139460096 | bytes 7303781 | solution.py:95
  134.7 3.4 gather_fusion.1
  140.8 18.2 %all_to_all.20 = bf16[2,384,768]{2,1,0:T(8,128)(2,1)S(1)} all-to-all(bf16[2,384,768]{2,1,0:T(8,128)(2,1)S(1)} %bitcast.258), channel_id=1, replica_groups=mesh['dp'=4,'seq'=4,'expert'=2] {'expert'}, dimensions={0} | all-to-all | bytes 2359296 | tf_op jit(solution)/shard_map/all_to_all | solution.py:117
  159.0 3.6 all-to-all-start.2
  162.9 8.6 %fusion.49 = f32[768,3072]{1,0:T(8,128)} fusion(bf16[768,768]{1,0:T(8,128)(2,1)S(1)} %bitcast.274, bf16[1,768,3072]{2,1,0:T(8,128)(2,1)} %all-gather.6.cloned.1.call-done), kind=kOutput, calls=%fused_computation.73 | convolution fusion | flops 3623878656 | bytes 15335424 | tf_op jit(solution)/shard_map/dot_general | solution.py:126
  171.5 5.9 all-to-all-done.2
  177.4 11.7 %fusion.42 = bf16[768,3072]{1,0:T(8,128)(2,1)S(1)} fusion(f32[768,3072]{1,0:T(8,128)} %fusion.49, bf16[768,768]{1,0:T(8,128)(2,1)S(1)} %bitcast.271, bf16[1,3072,768]{2,1,0:T(8,128)(2,1)} %all-gather.8.cloned.1.call-done), kind=kOutput, calls=%fused_computation.63 | convolution fusion | flops 3671064576 | bytes 20054016 | tf_op jit(solution)/shard_map/rd,fd->rf/dot_general | solution.py:147
  191.3 5.6 fusion.51
  198.2 8.9 %fusion.72 = bf16[768,768]{1,0:T(8,128)(2,1)} fusion(bf16[768,3072]{1,0:T(8,128)(2,1)} %copy-done.55, bf16[1,768,3072]{2,1,0:T(8,128)(2,1)} %all-gather.6.cloned.1.call-done), kind=kOutput, calls=%fused_computation.109 | convolution fusion | flops 3624468480 | bytes 10616832 | tf_op jit(solution)/shard_map/rf,df->rd/dot_general | solution.py:152
  207.0 4.1 all-to-all-start.3
  211.1 12.2 %fusion.75 = bf16[768,768]{1,0:T(8,128)(2,1)} fusion(bf16[1,3072,768]{2,1,0:T(8,128)(2,1)} %all-gather.8.cloned.1.call-done, f32[768,3072]{1,0:T(8,128)} %fusion.49), kind=kOutput, calls=%fused_computation.110 | convolution fusion | flops 3645702144 | bytes 15335424 | tf_op jit(solution)/shard_map/dot_general | solution.py:127
  224.8 3.6 all-to-all-start.1
  228.4 9.7 %fusion.52 = bf16[1,3072,768]{2,1,0:T(8,128)(2,1)} fusion(bf16[768,768]{1,0:T(8,128)(2,1)} %bitcast.272, f32[768,3072]{1,0:T(8,128)} %fusion.49), kind=kOutput, calls=%fused_computation.76 | convolution fusion | flops 3647471616 | bytes 15335424 | tf_op jit(solution)/shard_map/rf,rd->fd/dot_general | solution.py:144
  253.6 119.0 %while.29 = (s32[]{:T(128)}, bf16[12,2,256,64]{2,3,1,0:T(8,128)(2,1)S(1)}, f32[12,2,1024,64]{2,3,0,1:T(8,128)}, f32[12,2,1024,64]{2,3,0,1:T(8,128)}, bf16[12,2,2...) while((s32[]{:T(128)}, ...), condition=%wide.region_19.22_spmd.clone, body=%wide.region_17.21_spmd.clone.sunk | while | flops 341474816 | bytes 19423392 | solution.py:215
  372.6 11.9 %pad_maximum_fusion = f32[2,1024,1536]{1,2,0:T(8,128)} fusion(f32[2,1024,768]{1,2,0:T(8,128)} %bitcast.257, f32[2,1024,768]{1,2,0:T(8,128)} %bitcast.256), kind=kLoop, calls=%fused_computation.56 | loop fusion | flops 3145728 | bytes 25165824 | tf_op jit(solution)/shard_map/concatenate | solution.py:219
  391.6 92.8 %reduce-scatter.4.cloned.1.call-done = f32[2,256,1536]{1,2,0:T(8,128)} async-done(((f32[2,1024,1536]{1,2,0:T(8,128)}), f32[2,256,1536]{1,2,0:T(8,128)}) %reduce-scatter.4.cloned.1.call-update) | async-done | bytes 3145744 | tf_op jit(solution)/shard_map/reduce_scatter | solution.py:221
  489.4 3.9 fusion.79
  495.6 3.5 fusion.101
  499.1 83.8 %all-reduce.10.cloned.1.call-done = (bf16[1,768,768]{2,1,0:T(8,128)(2,1)}, bf16[1,768,768]{2,1,0:T(8,128)(2,1)}) async-done(((bf16[1,768,768]{2,1,0:T(8,128)(2,1)}, bf16[1,768,768]{2,1,0:T(8,128)(2,1)}), (bf16[1,768,768]{2,1,0:T(8,128)(2,1)}, bf16[1,768,768]{2,1,0:T(8,128)(2,1)})) %all-reduce.10.cloned.1.call-update) | async-done | bytes 2359312 | tf_op jit(solution)/shard_map/psum | solution.py:164
  592.9 41.6 %all-reduce.2 = (f32[768]{0:T(1024)}, f32[768]{0:T(1024)}) all-reduce(f32[768]{0:T(1024)} %get-tuple-element.224, f32[768]{0:T(1024)} %get-tuple-element.226), channel_id=1, replica_groups=mesh['dp'=4,'seq'=4,'expert'=2] {'dp','seq','expert'}, use_global_device_ids=true, to_apply=%region_24.27 | all-reduce | flops 1536 | bytes 12288 | tf_op jit(solution)/shard_map/psum | solution.py:247
  635.2 3.5 add_add_fusion.2
  638.7 143.1 %all-reduce.8.cloned.1.call-done = (f32[768,768]{1,0:T(8,128)}, f32[768,768]{1,0:T(8,128)}, f32[768,768]{1,0:T(8,128)}, f32[768,768]{1,0:T(8,128)}) async-done(((f32[768,768]{1,0:T(8,128)}, f32[768,768]{1,0:T(8,128)}, f32[768,768]{1,0:T(8,128)}, f32[768,768]{1,0:T(8,128)}), (f32[768,768]{1,0:T(8,128)}, f32[768,768]{1,0:T(8,128)}, f32[768,768]{1,0:T(8,128)}, ...) | async-done | bytes 9437200 | tf_op jit(solution)/shard_map/psum | solution.py:247
  (390 shorter events, 273.4 us)
Async XLA Ops:
  7.2 125.1 %copy-start = (bf16[768,768]{1,0:T(8,128)(2,1)S(1)}, bf16[768,768]{1,0:T(8,128)(2,1)}, u32[]{:S(2)}) copy-start(bf16[768,768]{1,0:T(8,128)(2,1)} %param.29) | copy-start | bytes 3538948
  7.2 4.2 copy-start.2
  7.2 4.2 copy-start.25
  7.2 61.7 %all-gather.4.cloned.1.call-start = ((), (), s32[]{:S(2)}) async-start(), calls=%async_computation.7 | async-start | bytes 7864320 | tf_op jit(solution)/shard_map/all_gather | solution.py:73
  11.8 19.7 %copy-start.10 = (bf16[512,768]{1,0:T(8,128)(2,1)}, bf16[512,768]{1,0:T(8,128)(2,1)S(1)}, u32[]{:S(2)}) copy-start(bf16[512,768]{1,0:T(8,128)(2,1)S(1)} %fusion.66) | copy-start | bytes 2359300
  18.8 3.9 copy-start.39
  18.8 4.0 copy-start.1
  18.9 144.1 %all-gather.6.cloned.1.call-start = ((), (), s32[]{:S(2)}) async-start(), calls=%async_computation.8 | async-start | bytes 5898240 | tf_op jit(solution)/shard_map/all_gather | solution.py:121
  19.6 151.9 %all-gather.8.cloned.1.call-start = ((), (), s32[]{:S(2)}) async-start(), calls=%async_computation.9 | async-start | bytes 5898240 | tf_op jit(solution)/shard_map/all_gather | solution.py:122
  27.1 7.4 copy-start.42
  134.7 3.5 copy-start.12
  134.7 3.5 copy-start.49
  159.0 18.4 %all-to-all-start.2 = ((bf16[2,384,768]{2,1,0:T(8,128)(2,1)}), bf16[2,384,768]{2,1,0:T(8,128)(2,1)S(1)}, u32[]{:S(2)}, u32[]{:S(2)}) async-start(bf16[2,384,768]{2,1,0:T(8,128)(2,1)} %bitcast.22), calls=%async_computation.2 | async-start | bytes 2359296 | tf_op jit(solution)/shard_map/all_to_all | solution.py:139
  162.6 222.0 %reduce-scatter.6.cloned.1.call-start = ((), (), s32[]{:S(2)}) async-start(), calls=%async_computation.11 | async-start | bytes 5898240 | tf_op jit(solution)/shard_map/reduce_scatter | solution.py:156
  177.4 11.7 %copy-start.21 = (bf16[2,384,768]{2,1,0:T(8,128)(2,1)}, bf16[2,384,768]{2,1,0:T(8,128)(2,1)S(1)}, u32[]{:S(2)}) copy-start(bf16[2,384,768]{2,1,0:T(8,128)(2,1)S(1)} %all-to-all-done.2) | copy-start | bytes 3538948
  207.0 17.8 %all-to-all-start.3 = ((bf16[2,384,768]{2,1,0:T(8,128)(2,1)}), bf16[2,384,768]{2,1,0:T(8,128)(2,1)S(1)}, u32[]{:S(2)}, u32[]{:S(2)}) async-start(bf16[2,384,768]{2,1,0:T(8,128)(2,1)} %bitcast.24), calls=%async_computation.3 | async-start | bytes 2359296 | tf_op jit(solution)/shard_map/all_to_all | solution.py:167
  224.8 19.2 %all-to-all-start.1 = ((bf16[2,384,768]{2,1,0:T(8,128)(2,1)}), bf16[2,384,768]{2,1,0:T(8,128)(2,1)S(1)}, u32[]{:S(2)}, u32[]{:S(2)}) async-start(bf16[2,384,768]{2,1,0:T(8,128)(2,1)} %bitcast.273), calls=%async_computation.1 | async-start | bytes 2359296 | tf_op jit(solution)/shard_map/all_to_all | solution.py:130
  228.4 156.3 %reduce-scatter.8.cloned.1.call-start = ((), (), s32[]{:S(2)}) async-start(), calls=%async_computation.12 | async-start | bytes 5898240 | tf_op jit(solution)/shard_map/reduce_scatter | solution.py:159
  238.1 246.4 %reduce-scatter.4.cloned.1.call-start = ((), (), s32[]{:S(2)}) async-start(), calls=%async_computation.10 | async-start | bytes 15728640 | tf_op jit(solution)/shard_map/reduce_scatter | solution.py:221
  246.7 3.4 copy-start.8
  384.5 198.4 %all-reduce.10.cloned.1.call-start = ((), (), s32[]{:S(2)}) async-start(), calls=%async_computation.14 | async-start | bytes 4718592 | tf_op jit(solution)/shard_map/psum | solution.py:164
  385.3 396.5 %all-reduce.8.cloned.1.call-start = ((), (), s32[]{:S(2)}) async-start(), calls=%async_computation.13 | async-start | bytes 18874368 | tf_op jit(solution)/shard_map/psum | solution.py:247
  489.4 98.1 %copy-start.6 = (bf16[2,256,1536]{2,1,0:T(8,128)(2,1)}, bf16[2,256,1536]{2,1,0:T(8,128)(2,1)S(1)}, u32[]{:S(2)}) copy-start(bf16[2,256,1536]{2,1,0:T(8,128)(2,1)S(1)} %copy.68) | copy-start | bytes 4718596
  489.4 3.9 copy-start.11
  (54 other events, 114.3 us)
Sparse Core Ops, SparseCore 0:
  18.9 49.8 all-gather.3
  70.4 37.4 all-gather.5
  109.5 37.4 all-gather.7
  197.1 47.0 reduce-scatter.5
  246.7 47.8 reduce-scatter.7
  384.6 99.8 reduce-scatter.3
  486.9 95.9 all-reduce.9
  589.7 192.0 all-reduce.7
where the time goes:
time: 806 us; the launch traced here: 799 us
  waiting for transfers between devices  355 us (44%)
  matrix products  219 us (27%)
  local copies, waits for them, and re-layouts  74.9 us (9%)
  other arithmetic  61.8 us (8%)
  blocking collectives  59.8 us (7%)
  between operations  15.2 us (2%)
  starting transfers between devices  12.2 us (2%)
    psum x1, waiting for transfers between devices, per_device(): lax.psum((grad_gain_attn, grad_w_query, grad_w_key, grad_w_value, grad_w_...  143 us
    reduce_scatter x1, waiting for transfers between devices, per_device(): lax.psum_scatter(pair_grads, 'seq', scatter_dimension=1, tiled=True)  92.8 us
    psum x1, waiting for transfers between devices, per_device(): lax.psum(grad_in_part.astype(jnp.bfloat16), 'dp').astype(jnp.float32)  83.8 us
    psum x1, blocking collectives, per_device(): lax.psum((grad_gain_attn, grad_w_query, grad_w_key, grad_w_value, grad_w_...  41.6 us
    all_gather x1, waiting for transfers between devices, per_device(): all_pairs = lax.all_gather(own_pair, 'seq', axis=1, tiled=True)  26.1 us
    dot_general x12, matrix products, head_backward(): jnp.einsum('rqd,rkd->rqk', query_one, key_one, preferred_element_type=jnp...  25.6 us
    unnamed x123, local copies, waits for them, and re-layouts  23.5 us
    dot_general x12, matrix products, head_backward(): jnp.einsum('rqk,rqd->rkd', grad_scores, query_one, preferred_element_type...  23.4 us
  transfers between devices with their start and end apart: 11, of which 6 were waited for; matrix products, arithmetic and copies ran while one was open for 39% of the time, Pallas kernels for 0%

commit v1 on v0

--- a/solution.py
+++ b/solution.py
@@ -1,14 +1,261 @@
+import functools
 import jax
 import jax.numpy as jnp
 from jax import lax
+from jax.experimental import pallas as pl
+from jax.experimental.pallas import tpu as pltpu
 from jax.sharding import PartitionSpec as P
 
+MESH = pl.DeviceIdType.MESH
+F32 = jnp.float32
+BF16 = jnp.bfloat16
 H = 12
 HD = 64
-
-
 epsilon = 1e-05
 masked_score = -1e30
+
+
+def dot_nn(a, b):
+    return jnp.dot(a, b, preferred_element_type=F32)
+
+
+def dot_nt(a, b):
+    return lax.dot_general(a, b, (((1,), (1,)), ((), ())), preferred_element_type=F32)
+
+
+def dot_tn(a, b):
+    return lax.dot_general(a, b, (((0,), (0,)), ((), ())), preferred_element_type=F32)
+
+
+def norm_stats(values):
+    average = jnp.mean(values, axis=-1, keepdims=True)
+    centred = values - average
+    spread = jnp.mean(centred * centred, axis=-1, keepdims=True)
+    return centred * lax.rsqrt(spread + epsilon)
+
+
+def attention_kernel(
+    tokens_hbm, lengths_ref, gain_ref, wq_ref, wk_ref, wv_ref, wo_ref,
+    middle_ref, att_ref, log_ref,
+    nb, wkt, wvt, qs, ks, vs, kt, vt, es, oa, stat, facs,
+    local_sem, tok_send, tok_recv, fwd_send, fwd_recv, core_send, core_recv,
+):
+    dp = lax.axis_index("dp")
+    s = lax.axis_index("seq")
+    y = lax.axis_index("expert")
+    c = lax.rem(s, 2)
+    x = s // 2
+    core_peer = (dp, x * 2 + 1 - c, y)
+    x_peer = (dp, (1 - x) * 2 + c, y)
+    span = tokens_hbm.shape[1]
+
+    own_copy = pltpu.make_async_copy(tokens_hbm, nb.at[s], local_sem)
+    own_copy.start()
+    barrier = pltpu.get_barrier_semaphore()
+    for peer in (core_peer, x_peer):
+        pl.semaphore_signal(barrier, inc=1, device_id=peer, device_id_type=MESH)
+    pl.semaphore_wait(barrier, 2)
+
+    def token_copy(r):
+        return pltpu.make_async_remote_copy(
+            src_ref=tokens_hbm.at[r], dst_ref=nb.at[s, r], send_sem=tok_send.at[r], recv_sem=tok_recv.at[r],
+            device_id=x_peer, device_id_type=MESH)
+
+    def core_copy(r):
+        return pltpu.make_async_remote_copy(
+            src_ref=tokens_hbm.at[r], dst_ref=nb.at[s, r], send_sem=core_send.at[r], recv_sem=core_recv.at[r],
+            device_id=core_peer, device_id_type=MESH)
+
+    def forward_copy(r):
+        return pltpu.make_async_remote_copy(
+            src_ref=nb.at[c, r], dst_ref=nb.at[c, r], send_sem=fwd_send.at[r], recv_sem=fwd_recv.at[r],
+            device_id=core_peer, device_id_type=MESH)
+
+    @pl.when(x == 0)
+    def _():
+        for r in range(2):
+            token_copy(r).start()
+
+    @pl.when(c == 0)
+    def _():
+        for r in range(2):
+            core_copy(r).start()
+
+    wkt[...] = wk_ref[...].T
+    wvt[...] = wv_ref[...].T
+    gain = gain_ref[...]
+
+    def normalise(part, r):
+        nb[part, r] = (norm_stats(nb[part, r].astype(F32)) * gain).astype(BF16)
+
+    def project(part, r):
+        normed = nb[part, r]
+        ks[part, r] = dot_nn(normed, wk_ref[...]).astype(BF16)
+        vs[part, r] = dot_nn(normed, wv_ref[...]).astype(BF16)
+        kt[part, r] = dot_nt(wkt[...], normed).astype(BF16)
+        vt[part, r] = dot_nt(wvt[...], normed).astype(BF16)
+
+    def attend(r, p, parts, diagonal):
+        lanes = pl.ds(pl.multiple_of(p * 128, 128), 128)
+        q_pair = qs[r, :, lanes]
+        first = lax.broadcasted_iota(jnp.int32, (span, 128), 1) < HD
+        results = []
+        for hh in range(2):
+            q_one = jnp.where(first if hh == 0 else jnp.logical_not(first), q_pair, jnp.zeros_like(q_pair))
+            scores = [dot_nt(ks[part, r, :, lanes], q_one) for part in parts]
+            if diagonal:
+                ki = lax.broadcasted_iota(jnp.int32, (span, span), 0)
+                qi = lax.broadcasted_iota(jnp.int32, (span, span), 1)
+                scores[-1] = jnp.where(ki <= qi, scores[-1], masked_score)
+            peak = jnp.max(scores[0], axis=0, keepdims=True)
+            for extra in scores[1:]:
+                peak = jnp.maximum(peak, jnp.max(extra, axis=0, keepdims=True))
+            total = 0.0
+            mixed = 0.0
+            h = 2 * p + hh
+            rows = pl.ds(pl.multiple_of(p * 128 + hh * HD, HD), HD)
+            for part, one in zip(parts, scores):
+                weights = jnp.exp(one - peak)
+                total = total + jnp.sum(weights, axis=0, keepdims=True)
+                low = weights.astype(BF16)
+                es[r, h, part] = low
+                mixed = mixed + dot_nn(vt[part, r, rows, :], low)
+            results.append((h, rows, peak, total, mixed))
+        return results
+
+    own_copy.wait()
+
+    def own_rows(r, carry):
+        normalise(s, r)
+        project(s, r)
+        qs[r] = (dot_nn(nb[s, r], wq_ref[...]) * (HD ** -0.5)).astype(BF16)
+        return carry
+
+    lax.fori_loop(0, 2, own_rows, 0)
+
+    def near(i, parts):
+        r, p = i // 6, lax.rem(i, 6)
+        for h, rows, peak, total, mixed in attend(r, p, parts, True):
+            stat[r, h, 0] = peak
+            stat[r, h, 1] = total
+            oa[r, rows, :] = mixed
+
+    @pl.when(c == 0)
+    def _():
+        def step(i, carry):
+            near(i, [s])
+            return carry
+        lax.fori_loop(0, 12, step, 0)
+
+    @pl.when(c == 1)
+    def _():
+        for r in range(2):
+            core_copy(r).wait_recv()
+
+        def partner_rows(r, carry):
+            normalise(s - 1, r)
+            project(s - 1, r)
+            return carry
+
+        lax.fori_loop(0, 2, partner_rows, 0)
+
+        def step(i, carry):
+            near(i, [s - 1, s])
+            return carry
+        lax.fori_loop(0, 12, step, 0)
+
+    @pl.when(x == 0)
+    def _():
+        def step(i, carry):
+            r, h = i // H, lax.rem(i, H)
+            rows = pl.ds(pl.multiple_of(h * HD, HD), HD)
+            inverse = 1.0 / stat[r, h, 1]
+            facs[r, h, 0] = inverse
+            facs[r, h, 1] = jnp.zeros_like(inverse)
+            log_ref[r, h] = stat[r, h, 0] + jnp.log(stat[r, h, 1])
+            oa[r, rows, :] = oa[r, rows, :] * inverse
+            return carry
+        lax.fori_loop(0, 2 * H, step, 0)
+
+    @pl.when(x == 1)
+    def _():
+        for r in range(2):
+            token_copy(r).wait_recv()
+            normalise(c, r)
+            forward_copy(r).start()
+            project(c, r)
+            forward_copy(r).wait()
+            project(1 - c, r)
+            single = lengths_ref[r, 1] == 0
+
+            def step(p, carry):
+                for h, rows, peak, total, mixed in attend(r, p, [0, 1], False):
+                    near_peak = stat[r, h, 0]
+                    peak = jnp.where(single, peak, near_peak)
+                    top = jnp.maximum(peak, near_peak)
+                    near_f = jnp.exp(near_peak - top)
+                    far_f = jnp.where(single, jnp.exp(peak - top), 0.0)
+                    whole = near_f * stat[r, h, 1] + far_f * total
+                    log_ref[r, h] = top + jnp.log(whole)
+                    near_f = near_f / whole
+                    far_f = far_f / whole
+                    facs[r, h, 0] = near_f
+                    facs[r, h, 1] = far_f
+                    oa[r, rows, :] = oa[r, rows, :] * near_f + mixed * far_f
+                return carry
+            lax.fori_loop(0, 6, step, 0)
+
+    def out_rows(r, carry):
+        att = oa[r].astype(BF16).T
+        att_ref[r] = att
+        middle_ref[r] = dot_nn(att, wo_ref[...])
+        return carry
+    lax.fori_loop(0, 2, out_rows, 0)
+
+    @pl.when(x == 0)
+    def _():
+        for r in range(2):
+            token_copy(r).wait_send()
+
+    @pl.when(c == 0)
+    def _():
+        for r in range(2):
+            core_copy(r).wait_send()
+
+
+def attention(tokens, lengths, gain, wq, wk, wv, wo):
+    rows, span, width = tokens.shape
+    vmem = pl.BlockSpec(memory_space=pltpu.VMEM)
+    sem = pltpu.SemaphoreType.DMA
+    blocks = (4, rows, span, width)
+    flipped = (4, rows, width, span)
+    return pl.pallas_call(
+        attention_kernel,
+        out_shape=(
+            jax.ShapeDtypeStruct((rows, span, width), F32),
+            jax.ShapeDtypeStruct((rows, span, width), BF16),
+            jax.ShapeDtypeStruct((rows, H, 1, span), F32),
+        ),
+        in_specs=[pl.BlockSpec(memory_space=pl.ANY), pl.BlockSpec(memory_space=pltpu.SMEM)] + [vmem] * 5,
+        out_specs=(vmem, vmem, vmem),
+        scratch_shapes=[
+            pltpu.VMEM(blocks, BF16),
+            pltpu.VMEM((width, width), BF16),
+            pltpu.VMEM((width, width), BF16),
+            pltpu.VMEM((rows, span, width), BF16),
+            pltpu.VMEM(blocks, BF16),
+            pltpu.VMEM(blocks, BF16),
+            pltpu.VMEM(flipped, BF16),
+            pltpu.VMEM(flipped, BF16),
+            pltpu.VMEM((rows, H, 4, span, span), BF16),
+            pltpu.VMEM((rows, width, span), F32),
+            pltpu.VMEM((rows, H, 2, 1, span), F32),
+            pltpu.VMEM((rows, H, 2, 1, span), F32),
+            sem, sem((2,)), sem((2,)), sem((2,)), sem((2,)), sem((2,)), sem((2,)),
+        ],
+        compiler_params=pltpu.CompilerParams(collective_id=1, has_side_effects=True, vmem_limit_bytes=60 << 20),
+        name="attention_forward",
+    )(tokens, lengths, gain.reshape(1, -1), wq, wk, wv, wo)
 
 
 def norm_rows(values, gain):
@@ -70,31 +317,15 @@
     keys = jnp.dot(normed_low, w_key, preferred_element_type=jnp.float32).astype(jnp.bfloat16)
     values = jnp.dot(normed_low, w_value, preferred_element_type=jnp.float32).astype(jnp.bfloat16)
     own_pair = jnp.concatenate([keys, values], axis=1).reshape(row_count, span, 2 * width)
-    all_pairs = lax.all_gather(own_pair, "seq", axis=1, tiled=True)
 
     def pair_heads(pairs):
         return (split_heads(pairs[:, :, :width]), split_heads(pairs[:, :, width:]))
 
     query_heads = split_heads(query.reshape(row_count, span, width))
-    key_heads, value_heads = pair_heads(all_pairs)
-
-    def head_forward(parts):
-        query_one, key_one, value_one = parts
-        scores = (
-            jnp.einsum("rqd,rkd->rqk", query_one, key_one, preferred_element_type=jnp.float32)
-            * scale
-        )
-        scores = jnp.where(visible, scores, masked_score)
-        peak = jnp.max(scores, axis=2, keepdims=True)
-        weights = jnp.exp(scores - peak)
-        totals = jnp.sum(weights, axis=2, keepdims=True)
-        probs = (weights / totals).astype(jnp.bfloat16)
-        mixed = jnp.einsum("rqk,rkd->rqd", probs, value_one, preferred_element_type=jnp.float32)
-        return (mixed, (peak + jnp.log(totals))[:, :, 0])
-
-    mixed_heads, log_totals = lax.map(head_forward, (query_heads, key_heads, value_heads))
-    attended = join_heads(mixed_heads).reshape(local_tok, width).astype(jnp.bfloat16)
-    middle = inputs + jnp.dot(attended, w_output, preferred_element_type=jnp.float32)
+    projected, attended, log_rows = attention(tokens, lengths, gain_attn, w_query, w_key, w_value, w_output)
+    attended = attended.reshape(local_tok, width)
+    log_totals = log_rows.transpose(1, 0, 2, 3).reshape(H, row_count, span)
+    middle = inputs + projected.reshape(local_tok, width)
     ffn_norm, second_norm_back = jax.vjp(norm_rows, middle, gain_ffn)
     ffn_in = ffn_norm.astype(jnp.bfloat16)
     experts = lax.axis_size("expert")

time: 806 us -> 777 us (0.964)
  matrix products: 219 us -> 164 us
  Pallas kernels: 0 us -> 40.4 us
  other arithmetic: 61.8 us -> 47.7 us
    dot_general x25 -> x0, matrix products: 41.7 us -> none  [the longest x12 22 us: head_forward(): jnp.einsum('rqd,rkd->rqk', query_one, key_one, preferred_element_type=jnp...]
    pallas_call x0 -> x1, Pallas kernels: none -> 40.4 us  [attention(): pl.pallas_call(attention_kernel, out_shape=(jax.ShapeDtypeStruct((rows, s...]
    all_gather x1, waiting for transfers between devices: 26.1 us -> 2.15 us  [per_device(): again_pairs = lax.all_gather(own_pair, 'seq', axis=1, tiled=True)]
    all_to_all x1, waiting for transfers between devices: 1.47 us -> 13.8 us  [per_device(): lax.all_to_all(grad_received.reshape(experts, capacity, width), 'expert',...]
    reduce_scatter x1, waiting for transfers between devices: 92.8 us -> 103 us  [per_device(): lax.psum_scatter(pair_grads, 'seq', scatter_dimension=1, tiled=True)]
    dot_general x12, matrix products: 23.4 us -> 13.3 us  [head_backward(): jnp.einsum('rqk,rqd->rkd', grad_scores, query_one, preferred_element_type...]
    unnamed x123 -> x117, local copies, waits for them, and re-layouts: 23.5 us -> 17.1 us
  transfers between devices with their start and end apart: 11 -> 11, of which waited for: 6 -> 8; matrix products, arithmetic and copies ran while one was open for 39% -> 31% of each run, Pallas kernels for 0% -> 5%
where the time goes in v1:
time: 777 us; the launch traced here: 766 us
  waiting for transfers between devices  358 us (46%)
  matrix products  164 us (21%)
  local copies, waits for them, and re-layouts  72.8 us (9%)
  blocking collectives  56 us (7%)
  other arithmetic  47.7 us (6%)
  Pallas kernels  40.4 us (5%)
  between operations  15.2 us (2%)
  starting transfers between devices  11.9 us (2%)
    psum x1, waiting for transfers between devices, per_device(): lax.psum((grad_gain_attn, grad_w_query, grad_w_key, grad_w_value, grad_w_...  145 us
    reduce_scatter x1, waiting for transfers between devices, per_device(): lax.psum_scatter(pair_grads, 'seq', scatter_dimension=1, tiled=True)  103 us
    psum x1, waiting for transfers between devices, per_device(): lax.psum(grad_in_part.astype(jnp.bfloat16), 'dp').astype(jnp.float32)  83.8 us
    psum x1, blocking collectives, per_device(): lax.psum((grad_gain_attn, grad_w_query, grad_w_key, grad_w_value, grad_w_...  41.4 us
    pallas_call x1, Pallas kernels, attention(): pl.pallas_call(attention_kernel, out_shape=(jax.ShapeDtypeStruct((rows, s...  40.4 us
    dot_general x12, matrix products, head_backward(): jnp.einsum('rqd,rkd->rqk', query_one, key_one, preferred_element_type=jnp...  25.3 us
    dot_general x12, matrix products, head_backward(): jnp.einsum('rqd,rkd->rqk', grad_one, value_one, preferred_element_type=jn...  17.2 us
    unnamed x117, local copies, waits for them, and re-layouts  17.1 us
  transfers between devices with their start and end apart: 11, of which 8 were waited for; matrix products, arithmetic and copies ran while one was open for 31% of the time, Pallas kernels for 5%

profile of v1, /device:TPU:0, one launch (start us, length us, event | category | flops | bytes accessed | tf_op | source)
XLA Modules:
  0.0 766.3 jit_solution(3675359936837427252)
XLA Ops:
  13.6 40.4 %attention_forward.1 = (f32[2,256,768]{2,1,0:T(8,128)}, bf16[2,256,768]{2,1,0:T(8,128)(2,1)}, f32[2,12,1,256]{3,2,1,0:T(1,128)}) custom-call(bf16[2,256,768]{2,1,0:T(8,128)(2,1)} %tokens_hbm.1, s32[2,2]{1,0:T(2,128)} %lengths_ref.1, f32[1,768]{1,0:T(1,128)} %reshape.355.gain_ref, bf16[768,768]{1,0:T(8,128)(2,1)} %wq_ref.1, bf16[768,768]{1,0:T(8,128)(2,1)} %wk_ref.1, ...), custom_call_target="tpu_custom_call" | custom-call | tf_op jit(solution)/shard_map/attention_forward/pallas_call | solution.py:232
  61.0 3.4 gather_fusion.3
  70.8 14.6 %all_to_all.20 = bf16[2,384,768]{2,1,0:T(8,128)(2,1)S(1)} all-to-all(bf16[2,384,768]{2,1,0:T(8,128)(2,1)S(1)} %bitcast.258), channel_id=1, replica_groups=mesh['dp'=4,'seq'=4,'expert'=2] {'expert'}, dimensions={0} | all-to-all | bytes 2359296 | tf_op jit(solution)/shard_map/all_to_all | solution.py:348
  85.3 3.6 all-to-all-start.2
  89.0 8.5 %fusion.32 = f32[768,3072]{1,0:T(8,128)} fusion(bf16[768,768]{1,0:T(8,128)(2,1)S(1)} %bitcast.269, bf16[1,768,3072]{2,1,0:T(8,128)(2,1)} %all-gather.4.cloned.1.call-done), kind=kOutput, calls=%fused_computation.54 | convolution fusion | flops 3623878656 | bytes 15335424 | tf_op jit(solution)/shard_map/dot_general | solution.py:357
  100.2 4.0 all-gather.6.cloned.1.call-done
  104.2 11.4 %fusion.25 = bf16[768,3072]{1,0:T(8,128)(2,1)S(1)} fusion(f32[768,3072]{1,0:T(8,128)} %fusion.32, bf16[768,768]{1,0:T(8,128)(2,1)S(1)} %bitcast.267, bf16[1,3072,768]{2,1,0:T(8,128)(2,1)} %all-gather.6.cloned.1.call-done), kind=kOutput, calls=%fused_computation.44 | convolution fusion | flops 3671064576 | bytes 20054016 | tf_op jit(solution)/shard_map/rd,fd->rf/dot_general | solution.py:378
  115.6 4.9 fusion.55
  120.5 3.9 all-to-all-start.3
  126.3 13.8 %all-to-all-done.3 = bf16[2,384,768]{2,1,0:T(8,128)(2,1)S(1)} async-done(((bf16[2,384,768]{2,1,0:T(8,128)(2,1)}), bf16[2,384,768]{2,1,0:T(8,128)(2,1)S(1)}, u32[]{:S(2)}, u32[]{:S(2)}) %all-to-all-start.3) | async-done | bytes 1179680 | tf_op jit(solution)/shard_map/all_to_all | solution.py:398
  153.5 7.8 %fusion.34 = bf16[1,768,3072]{2,1,0:T(8,128)(2,1)} fusion(bf16[768,768]{1,0:T(8,128)(2,1)S(1)} %bitcast.270, bf16[768,3072]{1,0:T(8,128)(2,1)} %copy-done.52), kind=kOutput, calls=%fused_computation.56 | convolution fusion | flops 3626237952 | bytes 10616832 | tf_op jit(solution)/shard_map/rd,rf->df/dot_general | solution.py:382
  165.1 11.5 %fusion.58 = bf16[768,768]{1,0:T(8,128)(2,1)} fusion(bf16[1,3072,768]{2,1,0:T(8,128)(2,1)} %all-gather.6.cloned.1.call-done, f32[768,3072]{1,0:T(8,128)} %fusion.32), kind=kOutput, calls=%fused_computation.92 | convolution fusion | flops 3645702144 | bytes 15335424 | tf_op jit(solution)/shard_map/dot_general | solution.py:358
  176.7 3.6 all-to-all-start.1
  180.6 9.8 %fusion.35 = bf16[1,3072,768]{2,1,0:T(8,128)(2,1)} fusion(bf16[768,768]{1,0:T(8,128)(2,1)} %bitcast.268, f32[768,3072]{1,0:T(8,128)} %fusion.32), kind=kOutput, calls=%fused_computation.57 | convolution fusion | flops 3647471616 | bytes 15335424 | tf_op jit(solution)/shard_map/rf,rd->fd/dot_general | solution.py:375
  198.7 3.5 fusion.81
  212.8 6.2 fusion.82
  219.1 109.2 %while.15 = (s32[]{:T(128)}, bf16[12,2,256,64]{2,3,1,0:T(8,128)(2,1)S(1)}, f32[12,2,1024,64]{2,3,0,1:T(8,128)}, f32[12,2,1024,64]{2,3,0,1:T(8,128)}, bf16[12,2,2...) while((s32[]{:T(128)}, ...), condition=%wide.region_15.18_spmd.clone, body=%wide.region_13.17_spmd.clone.sunk | while | flops 341474816 | bytes 18502812 | solution.py:446
  328.3 12.2 %pad_maximum_fusion = f32[2,1024,1536]{1,2,0:T(8,128)} fusion(f32[2,1024,768]{1,2,0:T(8,128)} %bitcast.256, f32[2,1024,768]{1,2,0:T(8,128)} %bitcast.257), kind=kLoop, calls=%fused_computation.37 | loop fusion | flops 3145728 | bytes 25165824 | tf_op jit(solution)/shard_map/concatenate | solution.py:450
  348.4 103.5 %reduce-scatter.4.cloned.1.call-done = f32[2,256,1536]{1,2,0:T(8,128)} async-done(((f32[2,1024,1536]{1,2,0:T(8,128)}), f32[2,256,1536]{1,2,0:T(8,128)}) %reduce-scatter.4.cloned.1.call-update) | async-done | bytes 3145744 | tf_op jit(solution)/shard_map/reduce_scatter | solution.py:452
  456.8 3.9 fusion.66
  462.9 3.5 fusion.83
  466.5 83.8 %all-reduce.10.cloned.1.call-done = (bf16[1,768,768]{2,1,0:T(8,128)(2,1)}, bf16[1,768,768]{2,1,0:T(8,128)(2,1)}) async-done(((bf16[1,768,768]{2,1,0:T(8,128)(2,1)}, bf16[1,768,768]{2,1,0:T(8,128)(2,1)}), (bf16[1,768,768]{2,1,0:T(8,128)(2,1)}, bf16[1,768,768]{2,1,0:T(8,128)(2,1)})) %all-reduce.10.cloned.1.call-update) | async-done | bytes 2359312 | tf_op jit(solution)/shard_map/psum | solution.py:395
  559.7 41.4 %all-reduce.2 = (f32[768]{0:T(1024)}, f32[768]{0:T(1024)}) all-reduce(f32[768]{0:T(1024)S(1)} %get-tuple-element.154, f32[768]{0:T(1024)S(1)} %copy-done.45), channel_id=1, replica_groups=mesh['dp'=4,'seq'=4,'expert'=2] {'dp','seq','expert'}, use_global_device_ids=true, to_apply=%region_20.23 | all-reduce | flops 1536 | bytes 12288 | tf_op jit(solution)/shard_map/psum | solution.py:478
  604.4 144.8 %all-reduce.8.cloned.1.call-done = (f32[768,768]{1,0:T(8,128)}, f32[768,768]{1,0:T(8,128)}, f32[768,768]{1,0:T(8,128)}, f32[768,768]{1,0:T(8,128)}) async-done(((f32[768,768]{1,0:T(8,128)}, f32[768,768]{1,0:T(8,128)}, f32[768,768]{1,0:T(8,128)}, f32[768,768]{1,0:T(8,128)}), (f32[768,768]{1,0:T(8,128)}, f32[768,768]{1,0:T(8,128)}, f32[768,768]{1,0:T(8,128)}, ...) | async-done | bytes 9437200 | tf_op jit(solution)/shard_map/psum | solution.py:478
  (308 shorter events, 206.6 us)
Async XLA Ops:
  7.2 81.8 %all-gather.4.cloned.1.call-start = ((), (), s32[]{:S(2)}) async-start(), calls=%async_computation.7 | async-start | bytes 5898240 | tf_op jit(solution)/shard_map/all_gather | solution.py:352
  7.9 5.0 copy-start.30
  7.9 96.2 %all-gather.6.cloned.1.call-start = ((), (), s32[]{:S(2)}) async-start(), calls=%async_computation.8 | async-start | bytes 5898240 | tf_op jit(solution)/shard_map/all_gather | solution.py:353
  13.6 40.5 %copy-start.2 = (bf16[2,256,768]{2,1,0:T(8,128)(2,1)S(1)}, bf16[2,256,768]{2,1,0:T(8,128)(2,1)}, u32[]{:S(2)}) copy-start(bf16[2,256,768]{2,1,0:T(8,128)(2,1)} %tokens_hbm.1) | copy-start | bytes 2359300
  58.3 6.1 copy-start.41
  85.3 12.1 %copy-start.21 = (bf16[2,384,768]{2,1,0:T(8,128)(2,1)}, bf16[2,384,768]{2,1,0:T(8,128)(2,1)S(1)}, u32[]{:S(2)}) copy-start(bf16[2,384,768]{2,1,0:T(8,128)(2,1)S(1)} %all_to_all.20) | copy-start | bytes 3538948
  85.3 14.9 %all-to-all-start.2 = ((bf16[2,384,768]{2,1,0:T(8,128)(2,1)}), bf16[2,384,768]{2,1,0:T(8,128)(2,1)S(1)}, u32[]{:S(2)}, u32[]{:S(2)}) async-start(bf16[2,384,768]{2,1,0:T(8,128)(2,1)} %bitcast.16), calls=%async_computation.2 | async-start | bytes 2359296 | tf_op jit(solution)/shard_map/all_to_all | solution.py:370
  100.2 15.4 %copy-start.20 = (bf16[2,384,768]{2,1,0:T(8,128)(2,1)}, bf16[2,384,768]{2,1,0:T(8,128)(2,1)S(1)}, u32[]{:S(2)}) copy-start(bf16[2,384,768]{2,1,0:T(8,128)(2,1)S(1)} %all-to-all-done.2) | copy-start | bytes 3538948
  104.2 11.4 %copy-start.51 = (bf16[1,768,3072]{2,1,0:T(8,128)(2,1)S(1)}, bf16[1,768,3072]{2,1,0:T(8,128)(2,1)}, u32[]{:S(2)}) copy-start(bf16[1,768,3072]{2,1,0:T(8,128)(2,1)} %all-gather.4.cloned.1.call-done) | copy-start | bytes 14155780
  115.6 4.9 copy-start.52
  120.5 19.6 %all-to-all-start.3 = ((bf16[2,384,768]{2,1,0:T(8,128)(2,1)}), bf16[2,384,768]{2,1,0:T(8,128)(2,1)S(1)}, u32[]{:S(2)}, u32[]{:S(2)}) async-start(bf16[2,384,768]{2,1,0:T(8,128)(2,1)} %bitcast.271), calls=%async_computation.3 | async-start | bytes 2359296 | tf_op jit(solution)/shard_map/all_to_all | solution.py:398
  124.4 88.4 %all-gather.8.cloned.1.call-start = ((), (), s32[]{:S(2)}) async-start(), calls=%async_computation.9 | async-start | bytes 7864320 | tf_op jit(solution)/shard_map/all_gather | solution.py:415
  152.3 188.6 %reduce-scatter.6.cloned.1.call-start = ((), (), s32[]{:S(2)}) async-start(), calls=%async_computation.11 | async-start | bytes 5898240 | tf_op jit(solution)/shard_map/reduce_scatter | solution.py:387
  176.7 18.5 %all-to-all-start.1 = ((bf16[2,384,768]{2,1,0:T(8,128)(2,1)}), bf16[2,384,768]{2,1,0:T(8,128)(2,1)S(1)}, u32[]{:S(2)}, u32[]{:S(2)}) async-start(bf16[2,384,768]{2,1,0:T(8,128)(2,1)} %bitcast.272), calls=%async_computation.1 | async-start | bytes 2359296 | tf_op jit(solution)/shard_map/all_to_all | solution.py:361
  180.3 160.6 %reduce-scatter.8.cloned.1.call-start = ((), (), s32[]{:S(2)}) async-start(), calls=%async_computation.12 | async-start | bytes 5898240 | tf_op jit(solution)/shard_map/reduce_scatter | solution.py:390
  190.4 261.4 %reduce-scatter.4.cloned.1.call-start = ((), (), s32[]{:S(2)}) async-start(), calls=%async_computation.10 | async-start | bytes 15728640 | tf_op jit(solution)/shard_map/reduce_scatter | solution.py:452
  210.7 8.4 %copy-start.26 = (bf16[12,2,256,64]{2,3,1,0:T(8,128)(2,1)S(1)}, bf16[12,2,256,64]{2,3,1,0:T(8,128)(2,1)}, u32[]{:S(2)}) copy-start(bf16[12,2,256,64]{2,3,1,0:T(8,128)(2,1)} %custom-call.10) | copy-start | bytes 2359300
  210.7 8.4 %copy-start.29 = (pred[256,1024]{1,0:T(8,128)(4,1)S(1)}, pred[256,1024]{1,0:T(8,128)(4,1)}, u32[]{:S(2)}) copy-start(pred[256,1024]{1,0:T(8,128)(4,1)} %iota_compare_fusion) | copy-start | bytes 786436
  210.7 8.4 %copy-start.47 = (s32[2,1024]{1,0:T(2,128)S(1)}, s32[2,1024]{1,0:T(2,128)}, u32[]{:S(2)}) copy-start(s32[2,1024]{1,0:T(2,128)} %fusion.70) | copy-start | bytes 24580
  210.7 8.4 %copy-start.50 = (s32[2,256]{1,0:T(2,128)S(1)}, s32[2,256]{1,0:T(2,128)}, u32[]{:S(2)}) copy-start(s32[2,256]{1,0:T(2,128)} %fusion.72) | copy-start | bytes 6148
  328.3 12.2 %copy-start.27 = (bf16[12,2,256,64]{2,3,1,0:T(8,128)(2,1)}, bf16[12,2,256,64]{2,3,1,0:T(8,128)(2,1)S(1)}, u32[]{:S(2)}) copy-start(bf16[12,2,256,64]{2,3,1,0:T(8,128)(2,1)S(1)} %get-tuple-element.71) | copy-start | bytes 2359300
  340.5 209.7 %all-reduce.10.cloned.1.call-start = ((), (), s32[]{:S(2)}) async-start(), calls=%async_computation.14 | async-start | bytes 4718592 | tf_op jit(solution)/shard_map/psum | solution.py:395
  341.3 407.9 %all-reduce.8.cloned.1.call-start = ((), (), s32[]{:S(2)}) async-start(), calls=%async_computation.13 | async-start | bytes 18874368 | tf_op jit(solution)/shard_map/psum | solution.py:478
  456.7 98.1 %copy-start.6 = (bf16[2,256,1536]{2,1,0:T(8,128)(2,1)}, bf16[2,256,1536]{2,1,0:T(8,128)(2,1)S(1)}, u32[]{:S(2)}) copy-start(bf16[2,256,1536]{2,1,0:T(8,128)(2,1)S(1)} %copy.60) | copy-start | bytes 4718596
  (40 other events, 78.3 us)
Sparse Core Ops, SparseCore 0:
  9.6 51.7 all-gather.3
  62.9 41.2 all-gather.5
  152.4 60.3 all-gather.7
  215.2 47.8 reduce-scatter.5
  265.7 47.8 reduce-scatter.7
  340.6 111.1 reduce-scatter.3
  454.3 95.9 all-reduce.9
  557.1 192.0 all-reduce.7

commit v2 on v1

--- a/solution.py
+++ b/solution.py
@@ -9,10 +9,13 @@
 MESH = pl.DeviceIdType.MESH
 F32 = jnp.float32
 BF16 = jnp.bfloat16
+I32 = jnp.int32
 H = 12
 HD = 64
 epsilon = 1e-05
 masked_score = -1e30
+gelu_a = 0.7978845608028654
+gelu_b = 0.044715
 
 
 def dot_nn(a, b):
@@ -27,18 +30,29 @@
     return lax.dot_general(a, b, (((0,), (0,)), ((), ())), preferred_element_type=F32)
 
 
-def norm_stats(values):
+def norm_parts(values):
     average = jnp.mean(values, axis=-1, keepdims=True)
     centred = values - average
     spread = jnp.mean(centred * centred, axis=-1, keepdims=True)
-    return centred * lax.rsqrt(spread + epsilon)
-
-
-def attention_kernel(
-    tokens_hbm, lengths_ref, gain_ref, wq_ref, wk_ref, wv_ref, wo_ref,
-    middle_ref, att_ref, log_ref,
-    nb, wkt, wvt, qs, ks, vs, kt, vt, es, oa, stat, facs,
-    local_sem, tok_send, tok_recv, fwd_send, fwd_recv, core_send, core_recv,
+    root = lax.rsqrt(spread + epsilon)
+    return centred * root, root
+
+
+def norm_back(upstream, gain, xhat, root):
+    scaled = upstream * gain
+    first = jnp.mean(scaled, axis=-1, keepdims=True)
+    second = jnp.mean(scaled * xhat, axis=-1, keepdims=True)
+    return root * (scaled - first - xhat * second)
+
+
+def block_kernel(
+    tokens_hbm, cot_ref, ids_ref, table_ref, lengths_ref, gain_a_ref, gain_f_ref,
+    wq_ref, wk_ref, wv_ref, wo_ref, win_hbm, wout_hbm,
+    out_hbm, ig_hbm, dwq_hbm, dwk_hbm, dwv_hbm, dwo_hbm, dwin_hbm, dwout_hbm, gg_ref, es_hbm,
+    nb, xgb, eob, qs, ks, vs, dot, ebuf, oa, stat, facs, dl, route, cs, xs, stage, do, mid,
+    win, wout, acc, preg, hid, gp, gback, eback, dnr0, dnr1,
+    local_sem, e_sem, tok_send, tok_recv, fwd_send, fwd_recv, core_send, core_recv,
+    wx_send, wx_recv, wc_send, wc_recv, y_send, y_recv, dn_send, dn_recv, dw_sem,
 ):
     dp = lax.axis_index("dp")
     s = lax.axis_index("seq")
@@ -47,85 +61,156 @@
     x = s // 2
     core_peer = (dp, x * 2 + 1 - c, y)
     x_peer = (dp, (1 - x) * 2 + c, y)
+    y_peer = (dp, s, 1 - y)
     span = tokens_hbm.shape[1]
-
-    own_copy = pltpu.make_async_copy(tokens_hbm, nb.at[s], local_sem)
+    width = tokens_hbm.shape[2]
+    local = 2 * span
+    cap = stage.shape[0]
+
+    def remote(src, dst, send, recv, peer):
+        return pltpu.make_async_remote_copy(
+            src_ref=src, dst_ref=dst, send_sem=send, recv_sem=recv, device_id=peer, device_id_type=MESH)
+
+    own_copy = pltpu.make_async_copy(tokens_hbm, nb.at[s], local_sem.at[0])
+    win_copy = pltpu.make_async_copy(win_hbm, win.at[s], local_sem.at[1])
+    wout_copy = pltpu.make_async_copy(wout_hbm, wout.at[s], local_sem.at[2])
     own_copy.start()
+    win_copy.start()
+    wout_copy.start()
     barrier = pltpu.get_barrier_semaphore()
-    for peer in (core_peer, x_peer):
+    for peer in (core_peer, x_peer, y_peer):
         pl.semaphore_signal(barrier, inc=1, device_id=peer, device_id_type=MESH)
-    pl.semaphore_wait(barrier, 2)
+    pl.semaphore_wait(barrier, 3)
+
+    far_s = (1 - x) * 2 + c
 
     def token_copy(r):
-        return pltpu.make_async_remote_copy(
-            src_ref=tokens_hbm.at[r], dst_ref=nb.at[s, r], send_sem=tok_send.at[r], recv_sem=tok_recv.at[r],
-            device_id=x_peer, device_id_type=MESH)
+        return remote(tokens_hbm.at[r], nb.at[s, r], tok_send.at[r], tok_recv.at[r], x_peer)
 
     def core_copy(r):
-        return pltpu.make_async_remote_copy(
-            src_ref=tokens_hbm.at[r], dst_ref=nb.at[s, r], send_sem=core_send.at[r], recv_sem=core_recv.at[r],
-            device_id=core_peer, device_id_type=MESH)
+        return remote(tokens_hbm.at[r], nb.at[s, r], core_send.at[r], core_recv.at[r], core_peer)
 
     def forward_copy(r):
-        return pltpu.make_async_remote_copy(
-            src_ref=nb.at[c, r], dst_ref=nb.at[c, r], send_sem=fwd_send.at[r], recv_sem=fwd_recv.at[r],
-            device_id=core_peer, device_id_type=MESH)
+        return remote(nb.at[c, r], nb.at[c, r], fwd_send.at[r], fwd_recv.at[r], core_peer)
+
+    wx_copies = [
+        remote(win_hbm, win.at[s], wx_send.at[0], wx_recv.at[0], x_peer),
+        remote(wout_hbm, wout.at[s], wx_send.at[1], wx_recv.at[1], x_peer),
+    ]
+    wc_copies = [
+        remote(win_hbm, win.at[s], wc_send.at[0], wc_recv.at[0], core_peer),
+        remote(wout_hbm, wout.at[s], wc_send.at[1], wc_recv.at[1], core_peer),
+        remote(win.at[far_s], win.at[far_s], wc_send.at[2], wc_recv.at[2], core_peer),
+        remote(wout.at[far_s], wout.at[far_s], wc_send.at[3], wc_recv.at[3], core_peer),
+    ]
 
     @pl.when(x == 0)
     def _():
         for r in range(2):
             token_copy(r).start()
 
+    @pl.when(x == 1)
+    def _():
+        for one in wx_copies:
+            one.start()
+
     @pl.when(c == 0)
     def _():
         for r in range(2):
             core_copy(r).start()
 
-    wkt[...] = wk_ref[...].T
-    wvt[...] = wv_ref[...].T
-    gain = gain_ref[...]
+    wc_copies[0].start()
+    wc_copies[1].start()
+
+    ids = jnp.concatenate([ids_ref[0:1, :], ids_ref[1:2, :]], axis=1)
+    high = ids // 128
+    low = ids - high * 128
+    pick = jnp.where(lax.broadcasted_iota(I32, (64, local), 0) == high, 1.0, 0.0).astype(BF16)
+    looked = dot_tn(table_ref[...].astype(F32).astype(BF16), pick)
+    expert_row = jnp.sum(
+        jnp.where(lax.broadcasted_iota(I32, (128, local), 0) == low, looked, 0.0), axis=0, keepdims=True)
+    mine = jnp.where(expert_row == y.astype(F32), 1.0, 0.0)
+    sixteen = lax.broadcasted_iota(I32, (16, local), 0)
+    both = jnp.where(sixteen == 0, mine, jnp.where(sixteen == 1, 1.0 - mine, 0.0)).astype(BF16)
+    before = jnp.where(
+        lax.broadcasted_iota(I32, (local, local), 0) < lax.broadcasted_iota(I32, (local, local), 1), 1.0, 0.0
+    ).astype(BF16)
+    ranks = dot_nn(both, before)
+    slot_rows = lax.broadcasted_iota(I32, (cap, local), 0).astype(F32)
+    for u in range(2):
+        chosen = mine if u == 0 else 1.0 - mine
+        route[u] = jnp.where(slot_rows == ranks[u:u + 1, :], chosen, 0.0).astype(BF16)
+
+    cot_copy = remote(stage, cs.at[cap:], y_send.at[0], y_recv.at[0], y_peer)
+    xs_copy = remote(stage, xs.at[cap:], y_send.at[1], y_recv.at[1], y_peer)
+    stage[...] = dot_nn(route[1], cot_ref[...]).astype(BF16)
+    cot_copy.start()
+    cs[0:cap] = dot_nn(route[0], cot_ref[...]).astype(BF16)
+
+    gain_a = gain_a_ref[...]
+    gain_f = gain_f_ref[...]
 
     def normalise(part, r):
-        nb[part, r] = (norm_stats(nb[part, r].astype(F32)) * gain).astype(BF16)
+        nb[part, r] = (norm_parts(nb[part, r].astype(F32))[0] * gain_a).astype(BF16)
 
     def project(part, r):
         normed = nb[part, r]
         ks[part, r] = dot_nn(normed, wk_ref[...]).astype(BF16)
         vs[part, r] = dot_nn(normed, wv_ref[...]).astype(BF16)
-        kt[part, r] = dot_nt(wkt[...], normed).astype(BF16)
-        vt[part, r] = dot_nt(wvt[...], normed).astype(BF16)
-
-    def attend(r, p, parts, diagonal):
-        lanes = pl.ds(pl.multiple_of(p * 128, 128), 128)
+
+    first_half = lax.broadcasted_iota(I32, (span, 128), 1) < HD
+    first_rows = lax.broadcasted_iota(I32, (128, span), 0) < HD
+
+    def only(values, keep, hh):
+        return jnp.where(keep if hh == 0 else jnp.logical_not(keep), values, jnp.zeros_like(values))
+
+    def pair_lanes(p):
+        return pl.ds(pl.multiple_of(p * 128, 128), 128)
+
+    def head_rows(p, hh):
+        return pl.ds(pl.multiple_of(p * 128 + hh * HD, HD), HD)
+
+    def e_near(r, p, slot, write, both_parts):
+        here = ebuf.at[slot] if both_parts else ebuf.at[slot, :, 1]
+        there = es_hbm.at[0, r, p] if both_parts else es_hbm.at[0, r, p, :, 1]
+        return pltpu.make_async_copy(here if write else there, there if write else here, e_sem.at[slot])
+
+    def e_far(r, p, slot, write):
+        here = ebuf.at[slot]
+        there = es_hbm.at[1, r, p]
+        return pltpu.make_async_copy(here if write else there, there if write else here, e_sem.at[slot])
+
+    def attend(r, p, slot, parts, places, diagonal):
+        lanes = pair_lanes(p)
         q_pair = qs[r, :, lanes]
-        first = lax.broadcasted_iota(jnp.int32, (span, 128), 1) < HD
+        v_flipped = [vs[part, r, :, lanes].T for part in parts]
         results = []
         for hh in range(2):
-            q_one = jnp.where(first if hh == 0 else jnp.logical_not(first), q_pair, jnp.zeros_like(q_pair))
+            q_one = only(q_pair, first_half, hh)
             scores = [dot_nt(ks[part, r, :, lanes], q_one) for part in parts]
             if diagonal:
-                ki = lax.broadcasted_iota(jnp.int32, (span, span), 0)
-                qi = lax.broadcasted_iota(jnp.int32, (span, span), 1)
+                ki = lax.broadcasted_iota(I32, (span, span), 0)
+                qi = lax.broadcasted_iota(I32, (span, span), 1)
                 scores[-1] = jnp.where(ki <= qi, scores[-1], masked_score)
             peak = jnp.max(scores[0], axis=0, keepdims=True)
             for extra in scores[1:]:
                 peak = jnp.maximum(peak, jnp.max(extra, axis=0, keepdims=True))
             total = 0.0
             mixed = 0.0
-            h = 2 * p + hh
-            rows = pl.ds(pl.multiple_of(p * 128 + hh * HD, HD), HD)
-            for part, one in zip(parts, scores):
+            rows = head_rows(p, hh)
+            for v_one, place, one in zip(v_flipped, places, scores):
                 weights = jnp.exp(one - peak)
                 total = total + jnp.sum(weights, axis=0, keepdims=True)
-                low = weights.astype(BF16)
-                es[r, h, part] = low
-                mixed = mixed + dot_nn(vt[part, r, rows, :], low)
-            results.append((h, rows, peak, total, mixed))
+                low_weights = weights.astype(BF16)
+                ebuf[slot, hh, place] = low_weights
+                mixed = mixed + dot_nn(v_one[hh * HD:(hh + 1) * HD], low_weights)
+            results.append((2 * p + hh, rows, peak, total, mixed))
         return results
 
     own_copy.wait()
 
     def own_rows(r, carry):
+        mid[r] = nb[s, r].astype(F32)
         normalise(s, r)
         project(s, r)
         qs[r] = (dot_nn(nb[s, r], wq_ref[...]) * (HD ** -0.5)).astype(BF16)
@@ -133,19 +218,30 @@
 
     lax.fori_loop(0, 2, own_rows, 0)
 
-    def near(i, parts):
-        r, p = i // 6, lax.rem(i, 6)
-        for h, rows, peak, total, mixed in attend(r, p, parts, True):
-            stat[r, h, 0] = peak
-            stat[r, h, 1] = total
-            oa[r, rows, :] = mixed
+    def near_loop(parts, places):
+        wide = len(parts) == 2
+
+        def step(i, carry):
+            r, p, slot = i // 6, lax.rem(i, 6), lax.rem(i, 2)
+
+            @pl.when(i >= 2)
+            def _():
+                e_near(r, p, slot, True, wide).wait()
+
+            for h, rows, peak, total, mixed in attend(r, p, slot, parts, places, True):
+                stat[r, h, 0] = peak
+                stat[r, h, 1] = total
+                oa[r, rows, :] = mixed
+            e_near(r, p, slot, True, wide).start()
+            return carry
+
+        lax.fori_loop(0, 12, step, 0)
+        for slot in range(2):
+            e_near(1, 4 + slot, slot, True, wide).wait()
 
     @pl.when(c == 0)
     def _():
-        def step(i, carry):
-            near(i, [s])
-            return carry
-        lax.fori_loop(0, 12, step, 0)
+        near_loop([s], [1])
 
     @pl.when(c == 1)
     def _():
@@ -158,23 +254,24 @@
             return carry
 
         lax.fori_loop(0, 2, partner_rows, 0)
-
-        def step(i, carry):
-            near(i, [s - 1, s])
-            return carry
-        lax.fori_loop(0, 12, step, 0)
+        near_loop([s - 1, s], [0, 1])
 
     @pl.when(x == 0)
     def _():
+        for r in range(2):
+            token_copy(r).wait_send()
+        for one in wx_copies:
+            one.start()
+
         def step(i, carry):
             r, h = i // H, lax.rem(i, H)
             rows = pl.ds(pl.multiple_of(h * HD, HD), HD)
             inverse = 1.0 / stat[r, h, 1]
             facs[r, h, 0] = inverse
             facs[r, h, 1] = jnp.zeros_like(inverse)
-            log_ref[r, h] = stat[r, h, 0] + jnp.log(stat[r, h, 1])
             oa[r, rows, :] = oa[r, rows, :] * inverse
             return carry
+
         lax.fori_loop(0, 2 * H, step, 0)
 
     @pl.when(x == 1)
@@ -189,33 +286,317 @@
             single = lengths_ref[r, 1] == 0
 
             def step(p, carry):
-                for h, rows, peak, total, mixed in attend(r, p, [0, 1], False):
+                slot = lax.rem(p, 2)
+
+                @pl.when(p >= 2)
+                def _():
+                    e_far(r, p, slot, True).wait()
+
+                for h, rows, peak, total, mixed in attend(r, p, slot, [0, 1], [0, 1], False):
                     near_peak = stat[r, h, 0]
                     peak = jnp.where(single, peak, near_peak)
                     top = jnp.maximum(peak, near_peak)
                     near_f = jnp.exp(near_peak - top)
                     far_f = jnp.where(single, jnp.exp(peak - top), 0.0)
                     whole = near_f * stat[r, h, 1] + far_f * total
-                    log_ref[r, h] = top + jnp.log(whole)
                     near_f = near_f / whole
                     far_f = far_f / whole
                     facs[r, h, 0] = near_f
                     facs[r, h, 1] = far_f
                     oa[r, rows, :] = oa[r, rows, :] * near_f + mixed * far_f
+                e_far(r, p, slot, True).start()
                 return carry
+
             lax.fori_loop(0, 6, step, 0)
+            for slot in range(2):
+                e_far(r, 4 + slot, slot, True).wait()
 
     def out_rows(r, carry):
         att = oa[r].astype(BF16).T
-        att_ref[r] = att
-        middle_ref[r] = dot_nn(att, wo_ref[...])
+        value = mid[r] + dot_nn(att, wo_ref[...])
+        mid[r] = value
+        do[0, r] = (norm_parts(value)[0] * gain_f).astype(BF16)
         return carry
+
     lax.fori_loop(0, 2, out_rows, 0)
 
+    ffn_in = do[0].reshape(local, width)
+    cot_copy.wait_send()
+    stage[...] = dot_nn(route[1], ffn_in).astype(BF16)
+    xs_copy.start()
+    xs[0:cap] = dot_nn(route[0], ffn_in).astype(BF16)
+    win_copy.wait()
+    wout_copy.wait()
+    acc[...] = jnp.zeros_like(acc)
+
+    def expert_rows(u, f):
+        rows = slice(u * cap, (u + 1) * cap)
+        preg[0] = dot_nn(xs[rows], win[f])
+        preg[1] = dot_nt(cs[rows], wout[f])
+
+        def gelu_rows(k, carry):
+            piece = pl.ds(pl.multiple_of(k * 16, 16), 16)
+            where = pl.ds(pl.multiple_of(u * cap + k * 16, 16), 16)
+            pre = preg[0, piece]
+            square = pre * pre
+            bent = jnp.tanh(gelu_a * pre * (1.0 + gelu_b * square))
+            half = 0.5 * (1.0 + bent)
+            slope = half + 0.5 * pre * (1.0 - bent * bent) * (gelu_a * (1.0 + 3.0 * gelu_b * square))
+            hid[f, where] = (pre * half).astype(BF16)
+            gp[f, where] = (preg[1, piece] * slope).astype(BF16)
+            return carry
+
+        lax.fori_loop(0, cap // 16, gelu_rows, 0, unroll=2)
+        acc[rows] += dot_nt(gp[f, rows], win[f])
+
+    def expert_number(ix, ic):
+        return 2 * lax.rem(x + ix, 2) + lax.rem(c + ic, 2)
+
+    def far_weights():
+        for k in range(2):
+            wx_copies[k].wait_recv()
+            wc_copies[2 + k].start()
+
+    for ix in range(2):
+        if ix == 1:
+            far_weights()
+        for u in range(2):
+            if ix == 0 and u == 1:
+                xs_copy.wait_recv()
+                cot_copy.wait_recv()
+
+            def two(ic, carry):
+                @pl.when(ic == 1)
+                def _():
+                    if u == 0:
+                        for k in range(2):
+                            wc_copies[2 * ix + k].wait_recv()
+                expert_rows(u, expert_number(ix, ic))
+                return carry
+
+            lax.fori_loop(0, 2, two, 0)
+
+    grad_copy = remote(xgb.at[cap:], gback, y_send.at[2], y_recv.at[2], y_peer)
+    out_copy = remote(eob.at[cap:], eback, y_send.at[3], y_recv.at[3], y_peer)
+    xgb[...] = acc[...].astype(BF16)
+    grad_copy.start()
+    acc[...] = jnp.zeros_like(acc)
+    wc_copies[0].wait_send()
+    wc_copies[1].wait_send()
+    wc_copies[2].wait_send()
+    wc_copies[3].wait_send()
+
+    def weight_grads(i, carry):
+        f = expert_number(1 - i // 2, lax.rem(i, 2))
+        acc[...] += dot_nn(hid[f], wout[f])
+        wout[f] = dot_tn(hid[f], cs[...]).astype(BF16)
+        win[f] = dot_tn(xs[...], gp[f]).astype(BF16)
+        pltpu.make_async_copy(wout.at[f], dwout_hbm.at[f], dw_sem.at[0, f]).start()
+        pltpu.make_async_copy(win.at[f], dwin_hbm.at[f], dw_sem.at[1, f]).start()
+        return carry
+
+    lax.fori_loop(0, 4, weight_grads, 0)
+    eob[...] = acc[...].astype(BF16)
+    out_copy.start()
+
+    grad_copy.wait_recv()
+    acc[...] = jnp.zeros_like(acc)
+    gg_ref[...] = jnp.zeros_like(gg_ref)
+
+    def take_back(r, own, returned):
+        picked = pl.ds(pl.multiple_of(r * span, span), span)
+        return dot_tn(route[0, :, picked], own) + dot_tn(route[1, :, picked], returned)
+
+    def ffn_back(r, carry):
+        rows = pl.ds(pl.multiple_of(r * span, span), span)
+        grad = take_back(r, xgb[0:cap], gback[...])
+        xhat, root = norm_parts(mid[r])
+        gg_ref[0:1] += jnp.sum(grad * xhat, axis=0, keepdims=True)
+        whole = cot_ref[rows].astype(F32) + norm_back(grad, gain_f, xhat, root)
+        preg_rows = preg.at[r, 0:span]
+        preg_rows[...] = whole
+        branch = whole.astype(BF16)
+        att = oa[r]
+        acc[...] += dot_nn(att.astype(BF16), branch)
+        up = dot_nt(wo_ref[...], branch)
+        up3 = up.reshape(H, HD, span)
+        inner = jnp.sum(up3 * att.reshape(H, HD, span), axis=1, keepdims=True)
+        for g in range(2):
+            factor = facs[r, :, g]
+            dl[r, :, g] = inner * factor
+            flipped = (up3 * factor).reshape(width, span).astype(BF16)
+            dot[g, r] = flipped
+            do[g, r] = flipped.T
+        oa[r] = jnp.zeros_like(oa[r])
+        return carry
+
+    lax.fori_loop(0, 2, ffn_back, 0)
+    dwo_out = pltpu.make_async_copy(xs, dwo_hbm, local_sem.at[3])
+    xs[...] = acc[...].astype(BF16)
+    dwo_out.start()
+
+    def attend_back(r, p, slot, g, parts, places):
+        lanes = pair_lanes(p)
+        q_pair = qs[r, :, lanes]
+        do_pair = do[g, r, :, lanes]
+        dot_pair = dot[g, r, lanes, :]
+        for part, place in zip(parts, places):
+            v_pair = vs[part, r, :, lanes]
+            k_flipped = ks[part, r, :, lanes].T
+            grad_k = 0.0
+            grad_v = 0.0
+            for hh in range(2):
+                h = 2 * p + hh
+                rows = head_rows(p, hh)
+                weights = ebuf[slot, hh, place]
+                grad_p = dot_nn(v_pair, only(dot_pair, first_rows, hh))
+                grad_s = (weights.astype(F32) * (grad_p - dl[r, h, g])).astype(BF16)
+                grad_v = grad_v + dot_nn(weights, only(do_pair, first_half, hh))
+                grad_k = grad_k + dot_nn(grad_s, only(q_pair, first_half, hh))
+                oa[r, rows, :] += dot_nn(k_flipped[hh * HD:(hh + 1) * HD], grad_s)
+            place_rows = pl.ds(pl.multiple_of(r * span, span), span)
+            hid[part, place_rows, lanes] = grad_k.astype(BF16)
+            gp[part, place_rows, lanes] = grad_v.astype(BF16)
+
+    def back_loop(g, parts, places):
+        wide = len(parts) == 2
+
+        def fetch(i):
+            r, p, slot = i // 6, lax.rem(i, 6), lax.rem(i, 2)
+            return e_near(r, p, slot, False, wide) if g == 0 else e_far(r, p, slot, False)
+
+        fetch(0).start()
+
+        def step(i, carry):
+            @pl.when(i < 11)
+            def _():
+                fetch(i + 1).start()
+            fetch(i).wait()
+            attend_back(i // 6, lax.rem(i, 6), lax.rem(i, 2), g, parts, places)
+            return carry
+
+        lax.fori_loop(0, 12, step, 0)
+
+    def normed_grad(part):
+        return dot_nt(hid[part, 0:local], wk_ref[...]) + dot_nt(gp[part, 0:local], wv_ref[...])
+
+    far_core = remote(cs.at[0:local], dnr0, dn_send.at[0], dn_recv.at[0], core_peer)
+    far_x = remote(cs.at[0:local], dnr0, dn_send.at[1], dn_recv.at[1], x_peer)
+    near_core = remote(xgb.at[0:local], dnr1, dn_send.at[2], dn_recv.at[2], core_peer)
+
+    @pl.when(x == 1)
+    def _():
+        back_loop(1, [0, 1], [0, 1])
+        cs[0:local] = normed_grad(1 - c).astype(BF16)
+        far_core.start()
+        mine_far = normed_grad(c)
+        far_core.wait()
+        cs[0:local] = (mine_far + dnr0[...].astype(F32)).astype(BF16)
+        far_x.start()
+
+    grad_copy.wait_send()
+
+    @pl.when(c == 0)
+    def _():
+        back_loop(0, [s], [1])
+
+    @pl.when(c == 1)
+    def _():
+        back_loop(0, [s - 1, s], [0, 1])
+        xgb[0:local] = normed_grad(s - 1).astype(BF16)
+        near_core.start()
+
+    out_copy.wait()
+
+    def out_add(r, carry):
+        rows = pl.ds(pl.multiple_of(r * span, span), span)
+        do[0, r] = (mid[r] + take_back(r, eob[0:cap], eback[...])).astype(BF16)
+        return carry
+
+    lax.fori_loop(0, 2, out_add, 0)
+    out_done = pltpu.make_async_copy(do.at[0], out_hbm, local_sem.at[4])
+    out_done.start()
+
+    tokens_again = pltpu.make_async_copy(tokens_hbm, do.at[1], local_sem.at[0])
+    tokens_again.start()
+    for r in range(2):
+        qs[r] = (oa[r] * (HD ** -0.5)).astype(BF16).T
+
+    def all_parts(grads):
+        acc[...] = jnp.zeros_like(acc)
+
+        def step(part, carry):
+            acc[...] += dot_tn(nb[part].reshape(local, width), grads[part, 0:local])
+            return carry
+
+        @pl.when(x == 1)
+        def _():
+            lax.fori_loop(0, 2, step, 0)
+
+        @pl.when(c == 1)
+        def _():
+            step(s - 1, 0)
+
+        step(s, 0)
+
+    all_parts(hid)
+    dwo_out.wait()
+    xs[...] = acc[...].astype(BF16)
+    dwk_out = pltpu.make_async_copy(xs, dwk_hbm, local_sem.at[3])
+    dwk_out.start()
+    all_parts(gp)
+    dwk_out.wait()
+    xs[...] = acc[...].astype(BF16)
+    dwv_out = pltpu.make_async_copy(xs, dwv_hbm, local_sem.at[3])
+    dwv_out.start()
+    query_grads = qs[...].reshape(local, width)
+    acc[...] = dot_tn(nb[s].reshape(local, width), query_grads)
+    dwv_out.wait()
+    xs[...] = acc[...].astype(BF16)
+    dwq_out = pltpu.make_async_copy(xs, dwq_hbm, local_sem.at[3])
+    dwq_out.start()
+    acc[0:local] = normed_grad(s) + dot_nt(query_grads, wq_ref[...])
+
+    @pl.when(c == 0)
+    def _():
+        near_core.wait_recv()
+        acc[0:local] += dnr1[...].astype(F32)
+
     @pl.when(x == 0)
     def _():
-        for r in range(2):
-            token_copy(r).wait_send()
+        far_x.wait_recv()
+        acc[0:local] += dnr0[...].astype(F32)
+
+    tokens_again.wait()
+
+    def first_back(r, carry):
+        rows = pl.ds(pl.multiple_of(r * span, span), span)
+        grad = acc[rows]
+        xhat, root = norm_parts(do[1, r].astype(F32))
+        gg_ref[1:2] += jnp.sum(grad * xhat, axis=0, keepdims=True)
+        mid[r] = preg[r, 0:span] + norm_back(grad, gain_a, xhat, root)
+        return carry
+
+    lax.fori_loop(0, 2, first_back, 0)
+    ig_done = pltpu.make_async_copy(mid, ig_hbm, local_sem.at[0])
+    ig_done.start()
+    ig_done.wait()
+    out_done.wait()
+    dwq_out.wait()
+    for f in range(4):
+        pltpu.make_async_copy(wout.at[f], dwout_hbm.at[f], dw_sem.at[0, f]).wait()
+        pltpu.make_async_copy(win.at[f], dwin_hbm.at[f], dw_sem.at[1, f]).wait()
+    xs_copy.wait_send()
+    for one in wx_copies:
+        one.wait_send()
+
+    @pl.when(x == 1)
+    def _():
+        far_x.wait_send()
+
+    @pl.when(c == 1)
+    def _():
+        near_core.wait_send()
 
     @pl.when(c == 0)
     def _():
@@ -223,39 +604,65 @@
             core_copy(r).wait_send()
 
 
-def attention(tokens, lengths, gain, wq, wk, wv, wo):
+def block(tokens, cot, ids, table, lengths, gain_a, gain_f, wq, wk, wv, wo, w_in, w_out):
     rows, span, width = tokens.shape
+    local = rows * span
+    cap = 3 * local // 4
     vmem = pl.BlockSpec(memory_space=pltpu.VMEM)
+    hbm = pl.BlockSpec(memory_space=pl.ANY)
+    smem = pl.BlockSpec(memory_space=pltpu.SMEM)
     sem = pltpu.SemaphoreType.DMA
+    square = (width, width)
     blocks = (4, rows, span, width)
-    flipped = (4, rows, width, span)
+    flipped = (2, rows, width, span)
+    shape = jax.ShapeDtypeStruct
     return pl.pallas_call(
-        attention_kernel,
+        block_kernel,
         out_shape=(
-            jax.ShapeDtypeStruct((rows, span, width), F32),
-            jax.ShapeDtypeStruct((rows, span, width), BF16),
-            jax.ShapeDtypeStruct((rows, H, 1, span), F32),
+            shape((rows, span, width), BF16),
+            shape((rows, span, width), F32),
+            shape(square, BF16), shape(square, BF16), shape(square, BF16), shape(square, BF16),
+            shape((4,) + square, BF16), shape((4,) + square, BF16),
+            shape((2, width), F32),
+            shape((2, rows, 6, 2, 2, span, span), BF16),
         ),
-        in_specs=[pl.BlockSpec(memory_space=pl.ANY), pl.BlockSpec(memory_space=pltpu.SMEM)] + [vmem] * 5,
-        out_specs=(vmem, vmem, vmem),
+        in_specs=[hbm, vmem, vmem, vmem, smem, vmem, vmem, vmem, vmem, vmem, vmem, hbm, hbm],
+        out_specs=(hbm,) * 8 + (vmem, hbm),
         scratch_shapes=[
             pltpu.VMEM(blocks, BF16),
-            pltpu.VMEM((width, width), BF16),
-            pltpu.VMEM((width, width), BF16),
+            pltpu.VMEM(square, BF16),
+            pltpu.VMEM(square, BF16),
             pltpu.VMEM((rows, span, width), BF16),
             pltpu.VMEM(blocks, BF16),
             pltpu.VMEM(blocks, BF16),
             pltpu.VMEM(flipped, BF16),
-            pltpu.VMEM(flipped, BF16),
-            pltpu.VMEM((rows, H, 4, span, span), BF16),
+            pltpu.VMEM((2, 2, 2, span, span), BF16),
             pltpu.VMEM((rows, width, span), F32),
             pltpu.VMEM((rows, H, 2, 1, span), F32),
             pltpu.VMEM((rows, H, 2, 1, span), F32),
-            sem, sem((2,)), sem((2,)), sem((2,)), sem((2,)), sem((2,)), sem((2,)),
+            pltpu.VMEM((rows, H, 2, 1, span), F32),
+            pltpu.VMEM((2, cap, local), BF16),
+            pltpu.VMEM((2 * cap, width), BF16),
+            pltpu.VMEM((2 * cap, width), BF16),
+            pltpu.VMEM((cap, width), BF16),
+            pltpu.VMEM((2, rows, span, width), BF16),
+            pltpu.VMEM((rows, span, width), F32),
+            pltpu.VMEM((4,) + square, BF16),
+            pltpu.VMEM((4,) + square, BF16),
+            pltpu.VMEM((2 * cap, width), F32),
+            pltpu.VMEM((2, cap, width), F32),
+            pltpu.VMEM((4, 2 * cap, width), BF16),
+            pltpu.VMEM((4, 2 * cap, width), BF16),
+            pltpu.VMEM((cap, width), BF16),
+            pltpu.VMEM((cap, width), BF16),
+            pltpu.VMEM((local, width), BF16),
+            pltpu.VMEM((local, width), BF16),
+            sem((5,)), sem((2,)), sem((2,)), sem((2,)), sem((2,)), sem((2,)), sem((2,)), sem((2,)),
+            sem((2,)), sem((2,)), sem((4,)), sem((4,)), sem((4,)), sem((4,)), sem((3,)), sem((3,)), sem((2, 4)),
         ],
         compiler_params=pltpu.CompilerParams(collective_id=1, has_side_effects=True, vmem_limit_bytes=60 << 20),
-        name="attention_forward",
-    )(tokens, lengths, gain.reshape(1, -1), wq, wk, wv, wo)
+        name="block_step",
+    )(tokens, cot, ids, table, lengths, gain_a, gain_f, wq, wk, wv, wo, w_in, w_out)
 
 
 def norm_rows(values, gain):
@@ -278,7 +685,7 @@
     return stacked.transpose(1, 2, 0, 3).reshape(stacked.shape[1], stacked.shape[2], H * HD)
 
 
-def per_device(
+def per_device_plain(
     tokens,
     token_ids,
     hash_table,
@@ -317,15 +724,31 @@
     keys = jnp.dot(normed_low, w_key, preferred_element_type=jnp.float32).astype(jnp.bfloat16)
     values = jnp.dot(normed_low, w_value, preferred_element_type=jnp.float32).astype(jnp.bfloat16)
     own_pair = jnp.concatenate([keys, values], axis=1).reshape(row_count, span, 2 * width)
+    all_pairs = lax.all_gather(own_pair, "seq", axis=1, tiled=True)
 
     def pair_heads(pairs):
         return (split_heads(pairs[:, :, :width]), split_heads(pairs[:, :, width:]))
 
     query_heads = split_heads(query.reshape(row_count, span, width))
-    projected, attended, log_rows = attention(tokens, lengths, gain_attn, w_query, w_key, w_value, w_output)
-    attended = attended.reshape(local_tok, width)
-    log_totals = log_rows.transpose(1, 0, 2, 3).reshape(H, row_count, span)
-    middle = inputs + projected.reshape(local_tok, width)
+    key_heads, value_heads = pair_heads(all_pairs)
+
+    def head_forward(parts):
+        query_one, key_one, value_one = parts
+        scores = (
+            jnp.einsum("rqd,rkd->rqk", query_one, key_one, preferred_element_type=jnp.float32)
+            * scale
+        )
+        scores = jnp.where(visible, scores, masked_score)
+        peak = jnp.max(scores, axis=2, keepdims=True)
+        weights = jnp.exp(scores - peak)
+        totals = jnp.sum(weights, axis=2, keepdims=True)
+        probs = (weights / totals).astype(jnp.bfloat16)
+        mixed = jnp.einsum("rqk,rkd->rqd", probs, value_one, preferred_element_type=jnp.float32)
+        return (mixed, (peak + jnp.log(totals))[:, :, 0])
+
+    mixed_heads, log_totals = lax.map(head_forward, (query_heads, key_heads, value_heads))
+    attended = join_heads(mixed_heads).reshape(local_tok, width).astype(jnp.bfloat16)
+    middle = inputs + jnp.dot(attended, w_output, preferred_element_type=jnp.float32)
     ffn_norm, second_norm_back = jax.vjp(norm_rows, middle, gain_ffn)
     ffn_in = ffn_norm.astype(jnp.bfloat16)
     experts = lax.axis_size("expert")
@@ -495,9 +918,50 @@
     )
 
 
+def per_device(
+    tokens,
+    token_ids,
+    hash_table,
+    lengths,
+    gain_attn,
+    w_query,
+    w_key,
+    w_value,
+    w_output,
+    gain_ffn,
+    w_in,
+    w_out,
+    cotangent,
+):
+    row_count, span, width = tokens.shape
+    local_tok = row_count * span
+    output, input_grad, grad_q, grad_k, grad_v, grad_o, part_in, part_out, gains, unused = block(
+        tokens, cotangent.reshape(local_tok, width), token_ids, hash_table.reshape(-1, 128), lengths,
+        gain_attn.reshape(1, width), gain_ffn.reshape(1, width),
+        w_query, w_key, w_value, w_output, w_in[0], w_out[0])
+    grad_in, grad_out = (
+        lax.psum(lax.psum_scatter(part, "seq", scatter_dimension=0, tiled=True), "dp").astype(F32)
+        for part in (part_in, part_out)
+    )
+    summed = lax.psum((grad_q, grad_k, grad_v, grad_o, gains), ("dp", "seq", "expert"))
+    return (
+        output,
+        input_grad,
+        summed[4][1],
+        summed[0].astype(F32),
+        summed[1].astype(F32),
+        summed[2].astype(F32),
+        summed[3].astype(F32),
+        summed[4][0],
+        grad_in,
+        grad_out,
+    )
+
+
 def solution(mesh):
+    sizes = (mesh.shape["dp"], mesh.shape["seq"], mesh.shape["expert"])
     return jax.shard_map(
-        per_device,
+        per_device if sizes == (4, 4, 2) else per_device_plain,
         mesh=mesh,
         in_specs=(
             P(("dp", "expert"), "seq", None),

time: 777 us -> 469 us (0.60)
  matrix products: 164 us -> 0 us
  waiting for transfers between devices: 358 us -> 240 us
  Pallas kernels: 40.4 us -> 147 us
  local copies, waits for them, and re-layouts: 72.8 us -> 6.85 us
  other arithmetic: 47.7 us -> 12.2 us
  blocking collectives: 56 us -> 39.5 us
  starting transfers between devices: 11.9 us -> 0.16 us
    dot_general x77 -> x0, matrix products: 164 us -> none  [the longest x12 25.3 us: head_backward(): jnp.einsum('rqd,rkd->rqk', query_one, key_one, preferred_element_type=jnp...]
    pallas_call x1, Pallas kernels: 40.4 us -> 147 us  [block(): pl.pallas_call(block_kernel, out_shape=(shape((rows, span, width), BF16),...]
    psum x2, waiting for transfers between devices: 229 us -> 130 us  [the longest x1 88.3 us: per_device(): lax.psum(lax.psum_scatter(part, 'seq', scatter_dimension=0, tiled=True),...]
    all_to_all x3 -> x0, waiting for transfers between devices: 18 us -> none  [the longest x1 13.8 us: per_device(): lax.all_to_all(grad_received.reshape(experts, capacity, width), 'expert',...]
    gather x5 -> x0, local copies, waits for them, and re-layouts: 15.8 us -> none  [the longest x2 6.88 us: to_slots(): return jnp.take(padded, sources, axis=0).reshape(experts, capacity, width)]
    all_to_all x1 -> x0, blocking collectives: 14.6 us -> none  [per_device(): lax.all_to_all(to_slots(ffn_in), 'expert', split_axis=0, concat_axis=0, t...]
    concatenate x2 -> x0, other arithmetic: 13.5 us -> none  [the longest x1 12.2 us: per_device(): jnp.concatenate([join_heads(grad_key_heads), join_heads(grad_value_heads)...]
    unnamed x117 -> x16, local copies, waits for them, and re-layouts: 17.1 us -> 3.7 us
  transfers between devices with their start and end apart: 11 -> 4, of which waited for: 8 -> 4; matrix products, arithmetic and copies ran while one was open for 31% -> 2% of each run, Pallas kernels for 5% -> 0%
where the time goes in v2:
time: 469 us; the launch traced here: 462 us
  waiting for transfers between devices  240 us (51%)
  Pallas kernels  147 us (31%)
  blocking collectives  39.5 us (8%)
  between operations  16 us (3%)
  other arithmetic  12.2 us (3%)
  local copies, waits for them, and re-layouts  6.85 us (1%)
    pallas_call x1, Pallas kernels, block(): pl.pallas_call(block_kernel, out_shape=(shape((rows, span, width), BF16),...  147 us
    reduce_scatter x2, waiting for transfers between devices, per_device(): lax.psum_scatter(part, 'seq', scatter_dimension=0, tiled=True)  108 us
    psum x1, waiting for transfers between devices, per_device(): lax.psum(lax.psum_scatter(part, 'seq', scatter_dimension=0, tiled=True),...  88.3 us
    psum x1, waiting for transfers between devices, per_device(): lax.psum((grad_q, grad_k, grad_v, grad_o, gains), ('dp', 'seq', 'expert'))  42 us
    psum x1, blocking collectives, per_device(): lax.psum((grad_q, grad_k, grad_v, grad_o, gains), ('dp', 'seq', 'expert'))  39.5 us
  transfers between devices with their start and end apart: 4, of which 4 were waited for; matrix products, arithmetic and copies ran while one was open for 2% of the time, Pallas kernels for 0%

profile of v2, /device:TPU:0, one launch (start us, length us, event | category | flops | bytes accessed | tf_op | source)
XLA Modules:
  0.0 462.1 jit_solution(12748176369113101945)
XLA Ops:
  8.1 1.3 reshape.34.gain_a_ref
  9.3 1.3 reshape.35.gain_f_ref
  10.6 147.4 %block_step.1 = (bf16[2,256,768]{2,1,0:T(8,128)(2,1)}, f32[2,256,768]{2,1,0:T(8,128)}, bf16[768,768]{1,0:T(8,128)(2,1)}, bf16[768,768]{1,0:T(8,128)(2,1)}, bf16[...) custom-call(bf16[2,256,768]{2,1,0:T(8,128)(2,1)} %tokens_hbm.1, ...), custom_call_target="tpu_custom_call" | custom-call | tf_op jit(solution)/shard_map/block_step/pallas_call | solution.py:619
  158.0 0.7 reduce-scatter.5.cloned.1.call-update
  158.7 0.0 all-reduce.5.cloned.1.call-start
  158.8 0.5 all-reduce.5.cloned.1.call-update
  159.4 56.4 %reduce-scatter.3.cloned.1.call-done = bf16[1,768,768]{2,1,0:T(8,128)(2,1)} async-done(((bf16[4,768,768]{2,1,0:T(8,128)(2,1)}), bf16[1,768,768]{2,1,0:T(8,128)(2,1)}) %reduce-scatter.3.cloned.1.call-update) | async-done | bytes 1179664 | tf_op jit(solution)/shard_map/reduce_scatter | solution.py:943
  215.8 52.0 %reduce-scatter.5.cloned.1.call-done = bf16[1,768,768]{2,1,0:T(8,128)(2,1)} async-done(((bf16[4,768,768]{2,1,0:T(8,128)(2,1)}), bf16[1,768,768]{2,1,0:T(8,128)(2,1)}) %reduce-scatter.5.cloned.1.call-update) | async-done | bytes 1179664 | tf_op jit(solution)/shard_map/reduce_scatter | solution.py:943
  267.8 0.7 copy-done.6
  268.5 39.5 %psum.49 = f32[2,768]{1,0:T(2,128)S(1)} all-reduce(f32[2,768]{1,0:T(2,128)S(1)} %copy-done.6), channel_id=1, replica_groups=mesh['dp'=4,'seq'=4,'expert'=2] {'dp','seq','expert'}, use_global_device_ids=true, to_apply=%region_0.0 | all-reduce | flops 1536 | bytes 12288 | tf_op jit(solution)/shard_map/psum | solution.py:946
  308.0 0.6 slice_reduce_fusion
  308.7 42.0 %all-reduce.5.cloned.1.call-done = (bf16[768,768]{1,0:T(8,128)(2,1)}, bf16[768,768]{1,0:T(8,128)(2,1)}, bf16[768,768]{1,0:T(8,128)(2,1)}, bf16[768,768]{1,0:T(8,128)(2,1)}) async-done(((bf16[768,768]{1,0:T(8,128)(2,1)}, bf16[768,768]{1,0:T(8,128)(2,1)}, bf16[768,768]{1,0:T(8,128)(2,1)}, bf16[768,768]{1,0:T(8,128)(2,1)}), (bf16[768,768]{1,0:T(8,128)(2,1)}, bf16[768,768]{1,0:T(8,128)(2,1)}, ...) | async-done | bytes 4718608 | tf_op jit(solution)/shard_map/psum | solution.py:946
  350.7 2.9 convert_element_type.18
  353.6 1.6 convert_element_type.19
  355.2 0.1 copy-done.2
  355.3 1.6 convert_element_type.20
  356.9 0.1 copy-done.1
  357.0 1.6 convert_element_type.21
  358.6 88.3 %all-reduce.7.cloned.1.call-done = (bf16[1,768,768]{2,1,0:T(8,128)(2,1)}, bf16[1,768,768]{2,1,0:T(8,128)(2,1)}) async-done(((bf16[1,768,768]{2,1,0:T(8,128)(2,1)}, bf16[1,768,768]{2,1,0:T(8,128)(2,1)}), (bf16[1,768,768]{2,1,0:T(8,128)(2,1)}, bf16[1,768,768]{2,1,0:T(8,128)(2,1)})) %all-reduce.7.cloned.1.call-update) | async-done | bytes 2359312 | tf_op jit(solution)/shard_map/psum | solution.py:943
  446.9 2.9 convert_element_type.22
  449.8 1.6 convert_element_type.23
  451.4 0.9 copy.31
  452.3 0.8 copy-done
  453.1 1.1 copy.32
  (15 shorter events, 0.2 us)
Async XLA Ops:
  8.0 207.8 %reduce-scatter.3.cloned.1.call-start = ((), (), s32[]{:S(2)}) async-start(), calls=%async_computation.2 | async-start | bytes 5898240 | tf_op jit(solution)/shard_map/reduce_scatter | solution.py:943
  158.0 109.8 %reduce-scatter.5.cloned.1.call-start = ((), (), s32[]{:S(2)}) async-start(), calls=%async_computation.3 | async-start | bytes 5898240 | tf_op jit(solution)/shard_map/reduce_scatter | solution.py:943
  158.7 191.9 %all-reduce.5.cloned.1.call-start = ((), (), s32[]{:S(2)}) async-start(), calls=%async_computation.4 | async-start | bytes 9437184 | tf_op jit(solution)/shard_map/psum | solution.py:946
  159.3 287.5 %all-reduce.7.cloned.1.call-start = ((), (), s32[]{:S(2)}) async-start(), calls=%async_computation.5 | async-start | bytes 4718592 | tf_op jit(solution)/shard_map/psum | solution.py:943
  267.8 0.7 copy-start.6
  350.7 2.9 copy-start.3
  353.6 1.7 copy-start.2
  355.3 1.7 copy-start.1
  446.9 2.9 copy-start.4
  449.8 1.6 copy-start.5
  451.4 1.7 copy-start
Sparse Core Ops, SparseCore 0:
  158.1 57.5 reduce-scatter.2
  218.3 49.4 reduce-scatter.4
Sparse Core Ops, SparseCore 1:
  165.4 185.3 all-reduce.4
  353.1 93.7 all-reduce.6
